TPU v7x, 32 devices: a whole 2x2x4 slice. The times are simulated.
32 devices in a mesh: dp: 2 (over core), expert: 16 (over z, y, x).
Axes of the slice: x: 2, y: 2, z: 4, core: 2. Of those that a mesh axis runs over, the one named last changes fastest.
Arguments:
- tokens: bfloat16 [32768, 768], P(('dp', 'expert')), may hold values from -6 to 6
- segments: int32 [32768], P(('dp', 'expert')), may hold values from 0 to 63, never falling along the last dimension, each value on 1 to 1024 neighbouring positions
- routes: int32 [32768, 1], P(('dp', 'expert')), may hold values from 0 to 15; in each aligned block of 1024 rows (0 to 1023, 1024 to 2047, ...) at most 128 rows name the same one
- capacity: int32 [16], replicated, may hold values from 64 to 128
- first_gain: bfloat16 [768], P('dp'), may hold values from 0.5 to 1.5
- query_weight: bfloat16 [768, 768], P('dp'), may hold values from -0.21875 to 0.21875
- key_weight: bfloat16 [768, 768], P('dp'), may hold values from -0.21875 to 0.21875
- value_weight: bfloat16 [768, 768], P('dp'), may hold values from -0.21875 to 0.21875
- output_weight: bfloat16 [768, 768], P('dp'), may hold values from -1.75 to 1.75
- position_bias: bfloat16 [32, 12], P('dp'), may hold values from -3 to 3
- second_gain: bfloat16 [768], P('dp'), may hold values from 0.5 to 1.5
- router_weight: bfloat16 [768, 16], P('dp'), may hold values from -0.15625 to 0.15625
- expert_up: bfloat16 [16, 768, 3072], P('expert', None, 'dp'), may hold values from -0.21875 to 0.21875
- expert_down: bfloat16 [16, 3072, 768], P('expert', 'dp'), may hold values from -0.109375 to 0.109375
- cotangent: bfloat16 [32768, 768], P(('dp', 'expert')), may hold values from -6 to 6
Outputs:
- layer_out: bfloat16 [32768, 768], P(('dp', 'expert'))
- input_grad: bfloat16 [32768, 768], P(('dp', 'expert'))
- first_grad: float32 [768], P(('dp', 'expert'))
- query_grad: float32 [768, 768], P(('dp', 'expert'))
- key_grad: float32 [768, 768], P(('dp', 'expert'))
- value_grad: float32 [768, 768], P(('dp', 'expert'))
- output_grad: float32 [768, 768], P(('dp', 'expert'))
- bias_grad: float32 [32, 12], replicated
- second_grad: float32 [768], P(('dp', 'expert'))
- router_grad: float32 [768, 16], P(('dp', 'expert'))
- up_grad: float32 [16, 768, 3072], P('expert', None, 'dp')
- down_grad: float32 [16, 3072, 768], P('expert', 'dp')
Inputs may be any that keep to these rules, and one draw needn't show every extreme that they name: `routes`: in each device's 1024 rows (an aligned block) no expert is named by more than 128 rows. `segments`: document numbers never fall along the tokens; a document has at most 1024 tokens.
All inputs are finite; a program needn't handle non-finite values.
Results may differ from a plain program's by a relative error of at most 0.014.
Values may be sent and summed in bfloat16 or wider, within the bound.
No kernel may reach another device: no remote copies, remote signals or barrier semaphores. Data moves between devices by JAX's collectives and lax.ppermute only.
A program may use at most 320 MiB of HBM per device.

v0:
```python
from functools import partial

import jax
import jax.numpy as jnp
import numpy as np
from jax import lax
from jax.sharding import PartitionSpec as P

D = 768
H = 12
HD = 64
BUCKETS = 32
MAXDIST = 128
LENGTH = 1024


epsilon = 1e-06


def bucket_table(length, buckets, max_reach):
    offsets = np.arange(-(length - 1), length)
    halved = buckets // 2
    linear = halved // 2
    upward = (offsets > 0).astype(np.int64) * halved
    distance = np.abs(offsets)
    scaled = (
        np.log(np.maximum(distance, 1) / linear) / np.log(max_reach / linear) * (halved - linear)
    )
    logpart = np.minimum(linear + np.floor(np.maximum(scaled, 0.0)).astype(np.int64), halved - 1)
    return (upward + np.where(distance < linear, distance, logpart)).astype(np.int32)


def bucket_matrix(length, buckets, max_reach):
    lookup = bucket_table(length, buckets, max_reach)
    across = np.arange(length)
    return lookup[across[None, :] - across[:, None] + length - 1]


def rms_norm(values, gain):
    return values * lax.rsqrt(jnp.mean(values * values, axis=-1, keepdims=True) + epsilon) * gain


def gate_values(logits, chosen):
    probability = jax.nn.softmax(logits, axis=-1)
    return logits.shape[-1] * jnp.sum(jnp.where(chosen, probability, 0.0), axis=-1)


def activation(values):
    return jax.nn.gelu(values, approximate=True)


def matmul(left, right):
    return jnp.dot(left, right, preferred_element_type=jnp.float32)


def matmul_tn(left, right):
    return lax.dot_general(
        left, right, (((0,), (0,)), ((), ())), preferred_element_type=jnp.float32
    )


def matmul_nt(left, right):
    return lax.dot_general(
        left, right, (((1,), (1,)), ((), ())), preferred_element_type=jnp.float32
    )


def block_onehot(bucket_ids, start, count):
    block_ids = jnp.asarray(bucket_ids[start : start + count])
    return (block_ids[None, :, :] == jnp.arange(BUCKETS, dtype=jnp.int32)[:, None, None]).astype(
        jnp.bfloat16
    )


def masked_scores(query_block, key_seq, segment_seq, relative, start):
    count = query_block.shape[0]
    scores = jnp.einsum(
        "qhd,khd->hqk", query_block, key_seq, preferred_element_type=jnp.float32
    ) * HD ** (-0.5)
    scores = scores + relative[:, start : start + count]
    same_doc = segment_seq[start : start + count, None] == segment_seq[None, :]
    return jnp.where(same_doc[None], scores, -1e30)


def shards(
    tokens,
    segments,
    routes,
    capacity,
    first_gain,
    query_weight,
    key_weight,
    value_weight,
    output_weight,
    position_bias,
    second_gain,
    router_weight,
    expert_up,
    expert_down,
    cotangent,
):
    (
        first_full,
        query_full,
        key_full,
        value_full,
        output_full,
        bias_full,
        second_full,
        router_full,
    ) = (
        lax.all_gather(first_gain, "dp", axis=0, tiled=True),
        lax.all_gather(query_weight, "dp", axis=0, tiled=True),
        lax.all_gather(key_weight, "dp", axis=0, tiled=True),
        lax.all_gather(value_weight, "dp", axis=0, tiled=True),
        lax.all_gather(output_weight, "dp", axis=0, tiled=True),
        lax.all_gather(position_bias, "dp", axis=0, tiled=True),
        lax.all_gather(second_gain, "dp", axis=0, tiled=True),
        lax.all_gather(router_weight, "dp", axis=0, tiled=True),
    )
    token_count = tokens.shape[0]
    sequences = token_count // LENGTH
    experts = router_full.shape[1]
    capacity_rows = max(2, 2 * token_count // experts)
    block_rows = min(512, LENGTH)
    bucket_ids = bucket_matrix(LENGTH, BUCKETS, MAXDIST)
    heads_shape = (sequences, LENGTH, H, HD)
    up_full, down_full = (
        lax.all_gather(expert_up, "dp", axis=2, tiled=True),
        lax.all_gather(expert_down, "dp", axis=1, tiled=True),
    )
    up_matrix = up_full[0]
    down_matrix = down_full[0]
    inputs = tokens.astype(jnp.float32)
    normed_attn, first_back = jax.vjp(rms_norm, inputs, first_full.astype(jnp.float32))
    attn_low = normed_attn.astype(jnp.bfloat16)
    queries = matmul(attn_low, query_full).astype(jnp.bfloat16)
    keys_all = matmul(attn_low, key_full).astype(jnp.bfloat16)
    values_all = matmul(attn_low, value_full).astype(jnp.bfloat16)
    relative = jnp.concatenate(
        [
            jnp.einsum(
                "ngo,ns->sgo",
                block_onehot(bucket_ids, start, block_rows),
                bias_full,
                preferred_element_type=jnp.float32,
            )
            for start in range(0, LENGTH, block_rows)
        ],
        axis=1,
    )
    segment_seqs = segments.reshape(sequences, LENGTH)

    def attend_one(pieces):
        query_seq, key_seq, value_seq, segment_seq = pieces
        outputs = []
        totals = []
        for start in range(0, LENGTH, block_rows):
            scores = masked_scores(
                query_seq[start : start + block_rows], key_seq, segment_seq, relative, start
            )
            largest = jnp.max(scores, axis=-1, keepdims=True)
            shifted = jnp.exp(scores - largest)
            denominator = jnp.sum(shifted, axis=-1, keepdims=True)
            weights = (shifted / denominator).astype(jnp.bfloat16)
            outputs.append(
                jnp.einsum("hqk,khd->qhd", weights, value_seq, preferred_element_type=jnp.float32)
            )
            totals.append(largest + jnp.log(denominator))
        return (jnp.concatenate(outputs, axis=0), jnp.concatenate(totals, axis=1))

    attended, log_totals = lax.map(
        attend_one,
        (
            queries.reshape(heads_shape),
            keys_all.reshape(heads_shape),
            values_all.reshape(heads_shape),
            segment_seqs,
        ),
    )
    heads_low = attended.reshape(token_count, D).astype(jnp.bfloat16)
    hidden = inputs + matmul(heads_low, output_full)
    normed_ffn, second_back = jax.vjp(rms_norm, hidden, second_full.astype(jnp.float32))
    ffn_low = normed_ffn.astype(jnp.bfloat16)
    logits = matmul(ffn_low, router_full)
    chosen_expert = routes[:, 0]
    chosen = chosen_expert[:, None] == jnp.arange(experts, dtype=jnp.int32)[None, :]
    gates, gate_back = jax.vjp(partial(gate_values, chosen=chosen), logits)
    earlier = jnp.cumsum(chosen.astype(jnp.int32), axis=0) - 1
    places = jnp.sum(jnp.where(chosen, earlier, 0), axis=1)
    limits = jnp.sum(jnp.where(chosen, capacity[None, :], 0), axis=1)
    kept = places < limits
    places = jnp.where(kept, places, capacity_rows)
    clipped = jnp.minimum(places, capacity_rows - 1)
    outgoing = (
        jnp.zeros((experts, capacity_rows, D), jnp.bfloat16)
        .at[chosen_expert, places]
        .set(ffn_low, mode="drop")
    )
    arrived = lax.all_to_all(outgoing, "expert", split_axis=0, concat_axis=0, tiled=True)
    used_rows = arrived
    before = matmul(used_rows.reshape(-1, D), up_matrix)
    produced = (
        matmul(activation(before).astype(jnp.bfloat16), down_matrix)
        .astype(jnp.bfloat16)
        .reshape(arrived.shape)
    )
    produced, used_rows, before = (
        produced,
        used_rows,
        before.reshape(used_rows.shape[0], used_rows.shape[1], -1),
    )
    returned = lax.all_to_all(produced, "expert", split_axis=0, concat_axis=0, tiled=True)
    results = (returned, used_rows, before)
    returned = results[0]
    used_rows = results[1]
    flat_rows = used_rows.reshape(-1, D)
    before_all = results[2].reshape(flat_rows.shape[0], -1)
    expert_rows = jnp.where(
        kept[:, None], returned[chosen_expert, clipped].astype(jnp.float32), 0.0
    )
    layer_out = (hidden + gates[:, None] * expert_rows).astype(jnp.bfloat16)
    grad_out = cotangent.astype(jnp.float32)
    grad_gates = jnp.sum(grad_out * expert_rows, axis=1)
    grad_sent = (gates[:, None] * grad_out).astype(jnp.bfloat16)
    grad_outgoing = (
        jnp.zeros((experts, capacity_rows, D), jnp.bfloat16)
        .at[chosen_expert, places]
        .set(grad_sent, mode="drop")
    )
    grad_arrived = lax.all_to_all(grad_outgoing, "expert", split_axis=0, concat_axis=0, tiled=True)
    grad_flat = grad_arrived.reshape(-1, D)
    activated, activation_back = jax.vjp(activation, before_all)
    grad_before = activation_back(matmul_nt(grad_flat, down_matrix))[0].astype(jnp.bfloat16)
    down_term = matmul_tn(activated.astype(jnp.bfloat16), grad_flat)
    up_term = matmul_tn(flat_rows, grad_before)
    grad_inputs = matmul_nt(grad_before, up_matrix)
    grad_back = grad_inputs.astype(jnp.bfloat16).reshape(grad_arrived.shape)
    up_grad, down_grad = (
        lax.psum_scatter(
            up_term[None].astype(jnp.bfloat16), "dp", scatter_dimension=2, tiled=True
        ).astype(jnp.float32),
        lax.psum_scatter(
            down_term[None].astype(jnp.bfloat16), "dp", scatter_dimension=1, tiled=True
        ).astype(jnp.float32),
    )
    grad_returned = lax.all_to_all(grad_back, "expert", split_axis=0, concat_axis=0, tiled=True)
    grad_experts = jnp.where(
        kept[:, None], grad_returned[chosen_expert, clipped].astype(jnp.float32), 0.0
    )
    grad_logits = gate_back(grad_gates)[0].astype(jnp.bfloat16)
    router_term = matmul_tn(ffn_low, grad_logits)
    grad_ffn = matmul_nt(grad_logits, router_full) + grad_experts
    grad_hidden, second_term = second_back(grad_ffn)
    grad_hidden = grad_hidden + grad_out
    grad_branch = grad_hidden.astype(jnp.bfloat16)
    output_term = matmul_tn(heads_low, grad_branch)
    grad_heads = matmul_nt(grad_branch, output_full).astype(jnp.bfloat16)

    def attend_back(pieces):
        query_seq, key_seq, value_seq, segment_seq, heads_grad, seq_totals = pieces
        grad_keys = jnp.zeros(key_seq.shape, jnp.float32)
        grad_values = jnp.zeros(value_seq.shape, jnp.float32)
        bias_term = jnp.zeros((BUCKETS, H), jnp.float32)
        query_parts = []
        for start in range(0, LENGTH, block_rows):
            query_block = query_seq[start : start + block_rows]
            grad_block = heads_grad[start : start + block_rows]
            scores = masked_scores(query_block, key_seq, segment_seq, relative, start)
            probability = jnp.exp(scores - seq_totals[:, start : start + block_rows])
            grad_probs = jnp.einsum(
                "qhd,khd->hqk", grad_block, value_seq, preferred_element_type=jnp.float32
            )
            grad_scores = (
                probability
                * (grad_probs - jnp.sum(probability * grad_probs, axis=-1, keepdims=True))
            ).astype(jnp.bfloat16)
            grad_values = grad_values + jnp.einsum(
                "hqk,qhd->khd",
                probability.astype(jnp.bfloat16),
                grad_block,
                preferred_element_type=jnp.float32,
            )
            query_parts.append(
                jnp.einsum("hqk,khd->qhd", grad_scores, key_seq, preferred_element_type=jnp.float32)
                * HD ** (-0.5)
            )
            grad_keys = grad_keys + jnp.einsum(
                "hqk,qhd->khd", grad_scores, query_block, preferred_element_type=jnp.float32
            ) * HD ** (-0.5)
            bias_term = bias_term + jnp.einsum(
                "pkm,fkm->fp",
                grad_scores,
                block_onehot(bucket_ids, start, block_rows),
                preferred_element_type=jnp.float32,
            )
        return (jnp.concatenate(query_parts, axis=0), grad_keys, grad_values, bias_term)

    grad_queries, grad_keys, grad_values, bias_terms = lax.map(
        attend_back,
        (
            queries.reshape(heads_shape),
            keys_all.reshape(heads_shape),
            values_all.reshape(heads_shape),
            segment_seqs,
            grad_heads.reshape(heads_shape),
            log_totals,
        ),
    )
    queries_low = grad_queries.reshape(token_count, D).astype(jnp.bfloat16)
    keys_low = grad_keys.reshape(token_count, D).astype(jnp.bfloat16)
    values_low = grad_values.reshape(token_count, D).astype(jnp.bfloat16)
    query_term = matmul_tn(attn_low, queries_low)
    key_term = matmul_tn(attn_low, keys_low)
    value_term = matmul_tn(attn_low, values_low)
    grad_attn = (
        matmul_nt(queries_low, query_full)
        + matmul_nt(keys_low, key_full)
        + matmul_nt(values_low, value_full)
    )
    grad_norm_in, first_term = first_back(grad_attn)
    input_grad = (grad_hidden + grad_norm_in).astype(jnp.bfloat16)
    first_grad, query_grad, key_grad, value_grad, output_grad, second_grad, router_grad = (
        lax.psum_scatter(first_term, ("dp", "expert"), scatter_dimension=0, tiled=True),
        lax.psum_scatter(query_term, ("dp", "expert"), scatter_dimension=0, tiled=True),
        lax.psum_scatter(key_term, ("dp", "expert"), scatter_dimension=0, tiled=True),
        lax.psum_scatter(value_term, ("dp", "expert"), scatter_dimension=0, tiled=True),
        lax.psum_scatter(output_term, ("dp", "expert"), scatter_dimension=0, tiled=True),
        lax.psum_scatter(second_term, ("dp", "expert"), scatter_dimension=0, tiled=True),
        lax.psum_scatter(router_term, ("dp", "expert"), scatter_dimension=0, tiled=True),
    )
    bias_grad = lax.psum(jnp.sum(bias_terms, axis=0), ("dp", "expert"))
    return (
        layer_out,
        input_grad,
        first_grad,
        query_grad,
        key_grad,
        value_grad,
        output_grad,
        bias_grad,
        second_grad,
        router_grad,
        up_grad,
        down_grad,
    )


def solution(mesh):
    placed = (
        P(("dp", "expert"), None),
        P(("dp", "expert")),
        P(("dp", "expert"), None),
        P(),
        P("dp"),
        P("dp", None),
        P("dp", None),
        P("dp", None),
        P("dp", None),
        P("dp", None),
        P("dp"),
        P("dp", None),
        P("expert", None, "dp"),
        P("expert", "dp", None),
        P(("dp", "expert"), None),
    )
    return jax.shard_map(
        shards,
        mesh=mesh,
        in_specs=placed,
        out_specs=(
            P(("dp", "expert"), None),
            P(("dp", "expert"), None),
            P(("dp", "expert")),
            P(("dp", "expert"), None),
            P(("dp", "expert"), None),
            P(("dp", "expert"), None),
            P(("dp", "expert"), None),
            P(),
            P(("dp", "expert")),
            P(("dp", "expert"), None),
            P("expert", None, "dp"),
            P("expert", "dp", None),
        ),
        check_vma=False,
    )
```

profile of v0, /device:TPU:0, one launch (start us, length us, event | category | flops | bytes accessed | tf_op | source)
XLA Modules:
  0.0 1107.9 jit_solution(15564406984749644776)
XLA Ops:
  16.5 16.7 %fusion.3 = f32[512,1024,12]{1,2,0:T(8,128)} fusion(s32[512,1024]{1,0:T(8,128)} %constant.105.clone, bf16[32,12]{1,0:T(8,128)(2,1)S(1)} %all_gather.34), kind=kOutput, calls=%fused_computation.9 | convolution fusion | flops 419430400 | bytes 27263744 | tf_op jit(solution)/shard_map/ngo,ns->sgo/dot_general | solution.py:142
  33.3 16.2 %fusion.1 = f32[512,1024,12]{1,2,0:T(8,128)} fusion(s32[512,1024]{1,0:T(8,128)S(1)} %copy-done.34, bf16[32,12]{1,0:T(8,128)(2,1)S(1)} %all_gather.34), kind=kOutput, calls=%fused_computation.6 | convolution fusion | flops 419430400 | bytes 27263744 | tf_op jit(solution)/shard_map/ngo,ns->sgo/dot_general | solution.py:142
  51.6 4.5 reduce-window.6
  61.9 3.1 convolution_convert_fusion.3
  65.0 30.3 %fusion.115 = (f32[12,512]{1,0:T(8,128)S(1)}, f32[12,512,1024]{2,1,0:T(8,128)}) fusion(f32[512,1024,12]{1,2,0:T(8,128)} %fusion.3, bf16[512,12,64]{0,2,1:T(8,128)(2,1)S(1)} %bitcast.151, bf16[1024,12,64]{0,2,1:T(8,128)(2,1)S(1)} %bitcast.143, pred[512,1024]{1,0:T(8,128)(4,1)S(1)} %get-tuple-element.141), kind=kOutput, calls=%fused_computation.173 | convolution fusion | flops 830466048 | bytes 53239808 | tf_op jit(solution)/shard_map/while/body/eval_jaxpr/qhd,khd->hqk/dot_general | solution.py:77
  95.3 11.1 %fusion.17 = f32[12,512]{1,0:T(8,128)S(1)} fusion(f32[12,512,1024]{2,1,0:T(8,128)} %get-tuple-element.148, f32[12,512]{1,0:T(8,128)S(1)} %get-tuple-element.147), kind=kLoop, calls=%fused_computation.38 | loop fusion | flops 12576768 | bytes 25214976 | tf_op jit(solution)/shard_map/while/body/eval_jaxpr/reduce_sum | solution.py:164
  109.3 11.1 fusion.69
  120.4 28.6 %fusion.114 = (f32[12,512]{1,0:T(8,128)S(1)}, f32[12,512,1024]{2,1,0:T(8,128)}) fusion(f32[512,1024,12]{1,2,0:T(8,128)} %fusion.1, bf16[512,12,64]{0,2,1:T(8,128)(2,1)S(1)} %bitcast.149, bf16[1024,12,64]{0,2,1:T(8,128)(2,1)S(1)} %bitcast.146, pred[512,1024]{1,0:T(8,128)(4,1)S(1)} %get-tuple-element.142), kind=kOutput, calls=%fused_computation.172 | convolution fusion | flops 830466048 | bytes 53239808 | tf_op jit(solution)/shard_map/while/body/eval_jaxpr/qhd,khd->hqk/dot_general | solution.py:77
  149.1 10.9 fusion.18
  160.0 10.8 fusion.70
  172.2 3.4 multiply_reduce_fusion.4
  178.3 7.3 scatter_custom_fusion
  185.6 8.1 all-to-all-start
  194.4 60.6 %all-to-all-done = bf16[16,128,768]{2,1,0:T(8,128)(2,1)S(1)} async-done(((bf16[16,128,768]{2,1,0:T(8,128)(2,1)}), bf16[16,128,768]{2,1,0:T(8,128)(2,1)S(1)}, u32[]{:S(2)}, u32[]{:S(2)}) %all-to-all-start) | async-done | bytes 3145760 | tf_op jit(solution)/shard_map/all_to_all | solution.py:200
  255.0 22.9 %multiply_convert_fusion.2 = (bf16[2048,3072]{1,0:T(8,128)(2,1)}, f32[2048,3072]{1,0:T(8,128)}) fusion(bf16[2048,768]{1,0:T(8,128)(2,1)S(1)} %bitcast.165, bf16[1,768,3072]{2,1,0:T(8,128)(2,1)} %all-gather.17.cloned.1.call-done), kind=kOutput, calls=%fused_computation.33 | convolution fusion | flops 9720299520 | bytes 45613056 | tf_op jit(solution)/shard_map/dot_general | solution.py:53
  277.9 15.4 %fusion.48 = bf16[2048,768]{1,0:T(8,128)(2,1)} fusion(bf16[2048,3072]{1,0:T(8,128)(2,1)} %get-tuple-element.153, bf16[1,3072,768]{2,1,0:T(8,128)(2,1)} %all-gather.19.cloned.1.call-done), kind=kOutput, calls=%fused_computation.75 | convolution fusion | flops 9665249280 | bytes 20447232 | tf_op jit(solution)/shard_map/dot_general | solution.py:53
  293.2 16.0 %all-to-all-start.1 = ((bf16[16,128,768]{2,1,0:T(8,128)(2,1)}), bf16[16,128,768]{2,1,0:T(8,128)(2,1)S(1)}, u32[]{:S(2)}, u32[]{:S(2)}) async-start(bf16[16,128,768]{2,1,0:T(8,128)(2,1)} %bitcast.168), calls=%async_computation.1 | async-start | bytes 6291456 | tf_op jit(solution)/shard_map/all_to_all | solution.py:213
  315.5 54.4 %all-to-all-done.1 = bf16[16,128,768]{2,1,0:T(8,128)(2,1)S(1)} async-done(((bf16[16,128,768]{2,1,0:T(8,128)(2,1)}), bf16[16,128,768]{2,1,0:T(8,128)(2,1)S(1)}, u32[]{:S(2)}, u32[]{:S(2)}) %all-to-all-start.1) | async-done | bytes 3145760 | tf_op jit(solution)/shard_map/all_to_all | solution.py:213
  369.9 14.1 %gather_fusion = bf16[1024,768]{1,0:T(8,128)(2,1)} fusion(bf16[16,128,768]{2,1,0:T(8,128)(2,1)S(1)} %all-to-all-done.1, s32[1024]{0:T(1024)S(1)} %bitcast.139), kind=kCustom, calls=%fused_computation | custom fusion | bytes 3153920 | tf_op jit(solution)/shard_map/gather | solution.py:220
  390.9 6.8 scatter_custom_fusion.1
  397.7 84.9 %all_to_all.20 = bf16[16,128,768]{2,1,0:T(8,128)(2,1)S(1)} all-to-all(bf16[16,128,768]{2,1,0:T(8,128)(2,1)S(1)} %bitcast.148), channel_id=1, replica_groups=mesh['dp'=2,'expert'=16] {'expert'}, dimensions={0} | all-to-all | bytes 6291456 | tf_op jit(solution)/shard_map/all_to_all | solution.py:231
  484.2 14.5 %fusion.42 = bf16[1,3072,768]{2,1,0:T(8,128)(2,1)} fusion(bf16[2048,3072]{1,0:T(8,128)(2,1)} %get-tuple-element.153, bf16[2048,768]{1,0:T(8,128)(2,1)S(1)} %bitcast.169), kind=kOutput, calls=%fused_computation.71 | convolution fusion | flops 9666035712 | bytes 20447232 | tf_op jit(solution)/shard_map/dot_general | solution.py:57
  500.7 27.9 %fusion.14 = bf16[2048,3072]{1,0:T(8,128)(2,1)} fusion(f32[2048,3072]{1,0:T(8,128)} %get-tuple-element.154, bf16[2048,768]{1,0:T(8,128)(2,1)S(1)} %bitcast.170, bf16[1,3072,768]{2,1,0:T(8,128)(2,1)} %all-gather.19.cloned.1.call-done), kind=kOutput, calls=%fused_computation.22 | convolution fusion | flops 9789505536 | bytes 45613056 | tf_op jit(solution)/shard_map/dot_general | solution.py:63
  528.6 15.9 %fusion.45 = bf16[2048,768]{1,0:T(8,128)(2,1)} fusion(bf16[2048,3072]{1,0:T(8,128)(2,1)} %fusion.14, bf16[1,768,3072]{2,1,0:T(8,128)(2,1)} %all-gather.17.cloned.1.call-done), kind=kOutput, calls=%fused_computation.74 | convolution fusion | flops 9665249280 | bytes 20447232 | tf_op jit(solution)/shard_map/dot_general | solution.py:63
  544.5 3.7 all-to-all-start.3
  548.3 15.3 %fusion.41 = bf16[1,768,3072]{2,1,0:T(8,128)(2,1)} fusion(bf16[2048,768]{1,0:T(8,128)(2,1)} %bitcast.166, bf16[2048,3072]{1,0:T(8,128)(2,1)} %fusion.14), kind=kOutput, calls=%fused_computation.70 | convolution fusion | flops 9666035712 | bytes 20447232 | tf_op jit(solution)/shard_map/dot_general | solution.py:57
  567.1 41.3 %all-to-all-done.3 = bf16[16,128,768]{2,1,0:T(8,128)(2,1)S(1)} async-done(((bf16[16,128,768]{2,1,0:T(8,128)(2,1)}), bf16[16,128,768]{2,1,0:T(8,128)(2,1)S(1)}, u32[]{:S(2)}, u32[]{:S(2)}) %all-to-all-start.3) | async-done | bytes 3145760 | tf_op jit(solution)/shard_map/all_to_all | solution.py:247
  608.4 14.2 %gather_fusion.1 = bf16[1024,768]{1,0:T(8,128)(2,1)} fusion(bf16[16,128,768]{2,1,0:T(8,128)(2,1)S(1)} %all-to-all-done.3, s32[1024]{0:T(1024)S(1)} %bitcast.140), kind=kCustom, calls=%fused_computation.1 | custom fusion | bytes 3153920 | tf_op jit(solution)/shard_map/gather | solution.py:249
  625.3 3.4 multiply_reduce_fusion.2
  636.7 19.8 %multiply_reduce_fusion.1 = (f32[12,512]{1,0:T(8,128)S(1)}, f32[12,512,1024]{2,1,0:T(8,128)}) fusion(f32[12,512,1024]{2,1,0:T(8,128)} %get-tuple-element.148, f32[12,512]{1,0:T(8,128)S(1)} %log_add_fusion.1, bf16[512,12,64]{0,2,1:T(8,128)(2,1)S(1)} %bitcast.153, bf16[1024,12,64]{0,2,1:T(8,128)(2,1)S(1)} %bitcast.160), kind=kOutput, calls=%fused_computation.31 | convolution fusion | flops 824174592 | bytes 52740096 | tf_op jit(solution)/shard_map/while/body/eval_jaxpr/qhd,khd->hqk/dot_general | solution.py:271
  656.5 16.6 %multiply_convert_fusion.1 = bf16[12,512,1024]{2,1,0:T(8,128)(2,1)S(1)} fusion(f32[12,512,1024]{2,1,0:T(8,128)} %get-tuple-element.159, f32[12,512,1024]{2,1,0:T(8,128)} %get-tuple-element.148, f32[12,512]{1,0:T(8,128)S(1)} %get-tuple-element.158, f32[12,512]{1,0:T(8,128)S(1)} %log_add_fusion.1), kind=kLoop, calls=%fused_computation.30 | loop fusion | flops 25165824 | bytes 62963712 | tf_op jit(solution)/shard_map/while/body/eval_jaxpr/convert_element_type | solution.py:277
  673.1 4.5 copy-done.3
  680.0 16.8 %multiply_reduce_fusion = (f32[12,512]{1,0:T(8,128)S(1)}, f32[12,512,1024]{2,1,0:T(8,128)}) fusion(f32[12,512,1024]{2,1,0:T(8,128)} %get-tuple-element.146, f32[12,512]{1,0:T(8,128)S(1)} %log_add_fusion, bf16[512,12,64]{0,2,1:T(8,128)(2,1)} %bitcast.155, bf16[1024,12,64]{0,2,1:T(8,128)(2,1)} %bitcast.159), kind=kOutput, calls=%fused_computation.28 | convolution fusion | flops 824174592 | bytes 52740096 | tf_op jit(solution)/shard_map/while/body/eval_jaxpr/qhd,khd->hqk/dot_general | solution.py:271
  696.8 17.2 %multiply_convert_fusion = bf16[12,512,1024]{2,1,0:T(8,128)(2,1)S(1)} fusion(f32[12,512,1024]{2,1,0:T(8,128)} %get-tuple-element.157, f32[12,512,1024]{2,1,0:T(8,128)} %get-tuple-element.146, f32[12,512]{1,0:T(8,128)S(1)} %get-tuple-element.156, f32[12,512]{1,0:T(8,128)S(1)} %log_add_fusion), kind=kLoop, calls=%fused_computation.27 | loop fusion | flops 25165824 | bytes 62963712 | tf_op jit(solution)/shard_map/while/body/eval_jaxpr/convert_element_type | solution.py:277
  723.5 10.1 fusion.67
  733.6 6.2 fusion.68
  742.7 2.9 fusion.106
  745.6 12.2 %fusion.23 = f32[12,64,1024]{2,1,0:T(8,128)} fusion(bf16[512,12,64]{0,2,1:T(8,128)(2,1)S(1)} %bitcast.156, f32[12,512,1024]{2,1,0:T(8,128)} %get-tuple-element.146, f32[12,512]{1,0:T(8,128)S(1)} %log_add_fusion), kind=kOutput, calls=%fused_computation.44 | convolution fusion | flops 817889280 | bytes 29122560 | tf_op jit(solution)/shard_map/while/body/eval_jaxpr/hqk,qhd->khd/dot_general | solution.py:278
  758.1 11.6 %add_convert_fusion = bf16[12,64,1024]{2,1,0:T(8,128)(2,1)S(1)} fusion(f32[12,64,1024]{2,1,0:T(8,128)} %fusion.23, bf16[512,12,64]{0,2,1:T(8,128)(2,1)S(1)} %bitcast.154, f32[12,512,1024]{2,1,0:T(8,128)} %get-tuple-element.148, f32[12,512]{1,0:T(8,128)S(1)} %log_add_fusion.1), kind=kOutput, calls=%fused_computation.85 | convolution fusion | flops 819462144 | bytes 30695424 | tf_op jit(solution)/shard_map/while/body/eval_jaxpr/hqk,qhd->khd/dot_general | solution.py:278
  773.8 21.3 %fusion.71 = f32[32,12]{0,1:T(8,128)S(1)} fusion(bf16[12,512,1024]{2,1,0:T(8,128)(2,1)} %copy-done.3, s32[512,1024]{1,0:T(8,128)} %constant.105.clone), kind=kOutput, calls=%fused_computation.112 | convolution fusion | flops 419430400 | bytes 14681600 | tf_op jit(solution)/shard_map/while/body/eval_jaxpr/pkm,fkm->fp/dot_general | solution.py:291
  799.5 3.7 fusion.52
  805.1 16.6 %fusion.77 = f32[32,12]{0,1:T(8,128)S(1)} fusion(f32[32,12]{0,1:T(8,128)S(1)} %fusion.71, bf16[12,512,1024]{2,1,0:T(8,128)(2,1)S(1)} %bitcast.142, s32[512,1024]{1,0:T(8,128)S(1)} %copy-done.35), kind=kOutput, calls=%fused_computation.114 | convolution fusion | flops 419430784 | bytes 14683136 | tf_op jit(solution)/shard_map/while/body/eval_jaxpr/pkm,fkm->fp/dot_general | solution.py:291
  821.7 50.8 %all-reduce.3 = (f32[768]{0:T(1024)S(1)}, f32[32,12]{0,1:T(8,128)}, f32[768]{0:T(1024)S(1)}, f32[768,16]{0,1:T(8,128)S(1)}) all-reduce(f32[768]{0:T(1024)S(1)} %get-tuple-element.122, f32[32,12]{0,1:T(8,128)S(1)} %fusion.77, f32[768]{0:T(1024)S(1)} %copy-done.65, ...), channel_id=2, replica_groups=mesh['dp'=2,'expert'=16] {'dp','expert'}, use_global_device_ids=true, to_apply=%region_22.23.clone | all-reduce | flops 14208 | bytes 113664
  873.7 3.7 fusion.56
  881.2 4.2 convert_element_type.184
  885.4 4.5 convert_element_type.181
  892.2 104.0 %reduce-scatter.8.cloned.1.call-done = f32[24,768]{1,0:T(8,128)} async-done(((f32[768,768]{1,0:T(8,128)}), f32[24,768]{1,0:T(8,128)}) %reduce-scatter.8.cloned.1.call-update) | async-done | bytes 73744 | tf_op jit(solution)/shard_map/reduce_scatter | solution.py:325
  996.2 104.6 %reduce-scatter.12.cloned.1.call-done = f32[24,768]{1,0:T(8,128)} async-done(((f32[768,768]{1,0:T(8,128)}), f32[24,768]{1,0:T(8,128)}) %reduce-scatter.12.cloned.1.call-update) | async-done | bytes 73744 | tf_op jit(solution)/shard_map/reduce_scatter | solution.py:327
  (265 shorter events, 87.4 us)
Async XLA Ops:
  7.2 50.9 %all-gather.11.cloned.1.call-start = ((), (), s32[]{:S(2)}) async-start(), calls=%async_computation.11 | async-start | bytes 1769472 | tf_op jit(solution)/shard_map/all_gather | solution.py:113
  7.9 54.0 %all-gather.13.cloned.1.call-start = ((), (), s32[]{:S(2)}) async-start(), calls=%async_computation.12 | async-start | bytes 1769472 | tf_op jit(solution)/shard_map/all_gather | solution.py:114
  8.7 97.8 %all-gather.9.cloned.1.call-start = ((), (), s32[]{:S(2)}) async-start(), calls=%async_computation.10 | async-start | bytes 1769472 | tf_op jit(solution)/shard_map/all_gather | solution.py:115
  9.4 162.8 %all-gather.15.cloned.1.call-start = ((), (), s32[]{:S(2)}) async-start(), calls=%async_computation.13 | async-start | bytes 1769472 | tf_op jit(solution)/shard_map/all_gather | solution.py:116
  10.0 184.4 %all-gather.17.cloned.1.call-start = ((), (), s32[]{:S(2)}) async-start(), calls=%async_computation.14 | async-start | bytes 7077888 | tf_op jit(solution)/shard_map/all_gather | solution.py:129
  12.3 159.9 %copy-start.6 = (bf16[1024,768]{0,1:T(8,128)(2,1)}, bf16[1024,768]{0,1:T(8,128)(2,1)S(1)}, u32[]{:S(2)}) copy-start(bf16[1024,768]{0,1:T(8,128)(2,1)S(1)} %copy.67) | copy-start | bytes 4718596
  12.7 20.6 %copy-start.59 = (f32[1024]{0:T(1024)}, f32[1024]{0:T(1024)S(1)}, u32[]{:S(2)}) copy-start(f32[1024]{0:T(1024)S(1)} %fusion.57) | copy-start | bytes 12292
  12.7 93.8 %copy-start.57 = (f32[1024]{0:T(1024)}, f32[1024]{0:T(1024)S(1)}, u32[]{:S(2)}) copy-start(f32[1024]{0:T(1024)S(1)} %fusion.97) | copy-start | bytes 12292
  14.7 91.8 %copy-start.55 = (f32[768]{0:T(1024)}, f32[768]{0:T(1024)S(1)}, u32[]{:S(2)}) copy-start(f32[768]{0:T(1024)S(1)} %reshape.315) | copy-start | bytes 9220
  16.5 16.7 %copy-start.34 = (s32[512,1024]{1,0:T(8,128)S(1)}, s32[512,1024]{1,0:T(8,128)}, u32[]{:S(2)}) copy-start(s32[512,1024]{1,0:T(8,128)} %constant.106.clone) | copy-start | bytes 6291460
  33.3 16.3 %copy-start.72 = (bf16[384]{0:T(512)(128)(2,1)S(1)}, bf16[384]{0:T(512)(128)(2,1)}, u32[]{:S(2)}) copy-start(bf16[384]{0:T(512)(128)(2,1)} %param.29) | copy-start | bytes 2308
  33.3 18.3 %copy-start.45 = (s32[1024,1]{0,1:T(1,128)S(1)}, s32[1024,1]{0,1:T(1,128)}, u32[]{:S(2)}) copy-start(s32[1024,1]{0,1:T(1,128)} %param.21) | copy-start | bytes 12292
  33.3 23.2 %copy-start.73 = (s32[16]{0:T(128)S(1)}, s32[16]{0:T(128)}, u32[]{:S(2)}) copy-start(s32[16]{0:T(128)} %param.22) | copy-start | bytes 196
  33.3 23.9 %copy-start.75 = (s32[2]{0:T(128)S(1)}, s32[2]{0:T(128)}, u32[]{:S(2)}) copy-start(s32[2]{0:T(128)} %constant.109) | copy-start | bytes 28
  33.3 24.0 %copy-start.74 = (s32[2]{0:T(128)S(1)}, s32[2]{0:T(128)}, u32[]{:S(2)}) copy-start(s32[2]{0:T(128)} %constant.112) | copy-start | bytes 28
  51.5 124.2 %copy-start.51 = (f32[768]{0:T(1024)}, f32[768]{0:T(1024)S(1)}, u32[]{:S(2)}) copy-start(f32[768]{0:T(1024)S(1)} %reshape.316) | copy-start | bytes 9220
  61.9 58.5 %copy-start.17 = (bf16[512,768]{0,1:T(8,128)(2,1)}, bf16[512,768]{0,1:T(8,128)(2,1)S(1)}, u32[]{:S(2)}) copy-start(bf16[512,768]{0,1:T(8,128)(2,1)S(1)} %get-tuple-element.137) | copy-start | bytes 2359300
  65.0 30.3 %copy-start.12 = (bf16[1024,768]{0,1:T(8,128)(2,1)}, bf16[1024,768]{0,1:T(8,128)(2,1)S(1)}, u32[]{:S(2)}) copy-start(bf16[1024,768]{0,1:T(8,128)(2,1)S(1)} %convolution_convert_fusion.3) | copy-start | bytes 4718596
  95.3 14.0 %copy-start.40 = (f32[12,512]{1,0:T(8,128)}, f32[12,512]{1,0:T(8,128)S(1)}, u32[]{:S(2)}) copy-start(f32[12,512]{1,0:T(8,128)S(1)} %get-tuple-element.147) | copy-start | bytes 73732
  109.3 50.7 %copy-start.24 = (bf16[1024,768]{0,1:T(8,128)(2,1)}, bf16[1024,768]{0,1:T(8,128)(2,1)S(1)}, u32[]{:S(2)}) copy-start(bf16[1024,768]{0,1:T(8,128)(2,1)S(1)} %convolution_convert_fusion.5) | copy-start | bytes 4718596
  109.3 11.1 %copy-start.13 = (bf16[1024,768]{0,1:T(8,128)(2,1)S(1)}, bf16[1024,768]{0,1:T(8,128)(2,1)}, u32[]{:S(2)}) copy-start(bf16[1024,768]{0,1:T(8,128)(2,1)} %copy-done.12) | copy-start | bytes 4718596
  149.1 10.9 copy-start.42
  160.0 10.8 copy-start.49
  177.6 8.0 copy-start.9
  185.6 69.3 %all-to-all-start = ((bf16[16,128,768]{2,1,0:T(8,128)(2,1)}), bf16[16,128,768]{2,1,0:T(8,128)(2,1)S(1)}, u32[]{:S(2)}, u32[]{:S(2)}) async-start(bf16[16,128,768]{2,1,0:T(8,128)(2,1)} %bitcast.147), calls=%async_computation | async-start | bytes 6291456 | tf_op jit(solution)/shard_map/all_to_all | solution.py:200
  193.8 84.1 %all-gather.19.cloned.1.call-start = ((), (), s32[]{:S(2)}) async-start(), calls=%async_computation.15 | async-start | bytes 7077888 | tf_op jit(solution)/shard_map/all_gather | solution.py:130
  255.0 22.9 %copy-start.31 = (bf16[16,128,768]{2,1,0:T(8,128)(2,1)}, bf16[16,128,768]{2,1,0:T(8,128)(2,1)S(1)}, u32[]{:S(2)}) copy-start(bf16[16,128,768]{2,1,0:T(8,128)(2,1)S(1)} %all-to-all-done) | copy-start | bytes 9437188
  293.2 16.1 %copy-start.62 = (s32[1024]{0:T(1024)S(1)}, s32[1024]{0:T(1024)}, u32[]{:S(2)}) copy-start(s32[1024]{0:T(1024)} %copy-done.61) | copy-start | bytes 12292
  293.2 16.1 %copy-start.64 = (s32[1024]{0:T(1024)S(1)}, s32[1024]{0:T(1024)}, u32[]{:S(2)}) copy-start(s32[1024]{0:T(1024)} %copy-done.63) | copy-start | bytes 12292
  293.2 76.7 %all-to-all-start.1 = ((bf16[16,128,768]{2,1,0:T(8,128)(2,1)}), bf16[16,128,768]{2,1,0:T(8,128)(2,1)S(1)}, u32[]{:S(2)}, u32[]{:S(2)}) async-start(bf16[16,128,768]{2,1,0:T(8,128)(2,1)} %bitcast.168), calls=%async_computation.1 | async-start | bytes 6291456 | tf_op jit(solution)/shard_map/all_to_all | solution.py:213
  309.2 60.7 %copy-start = (s32[1024,1]{0,1:T(1,128)S(1)}, s32[1024,1]{0,1:T(1,128)}, u32[]{:S(2)}) copy-start(s32[1024,1]{0,1:T(1,128)} %get-tuple-element.138) | copy-start | bytes 12292
  309.3 572.0 %reduce-scatter.18.cloned.1.call-start = ((), (), s32[]{:S(2)}) async-start(), calls=%async_computation.21 | async-start | bytes 7077888 | tf_op jit(solution)/shard_map/reduce_scatter | solution.py:243
  544.5 63.8 %all-to-all-start.3 = ((bf16[16,128,768]{2,1,0:T(8,128)(2,1)}), bf16[16,128,768]{2,1,0:T(8,128)(2,1)S(1)}, u32[]{:S(2)}, u32[]{:S(2)}) async-start(bf16[16,128,768]{2,1,0:T(8,128)(2,1)} %bitcast.167), calls=%async_computation.3 | async-start | bytes 6291456 | tf_op jit(solution)/shard_map/all_to_all | solution.py:247
  548.3 337.1 %reduce-scatter.16.cloned.1.call-start = ((), (), s32[]{:S(2)}) async-start(), calls=%async_computation.20 | async-start | bytes 7077888 | tf_op jit(solution)/shard_map/reduce_scatter | solution.py:240
  563.7 326.2 %reduce-scatter.14.cloned.1.call-start = ((), (), s32[]{:S(2)}) async-start(), calls=%async_computation.19 | async-start | bytes 2433024 | tf_op jit(solution)/shard_map/reduce_scatter | solution.py:328
  608.4 16.9 %copy-start.52 = (f32[768]{0:T(1024)S(1)}, f32[768]{0:T(1024)}, u32[]{:S(2)}) copy-start(f32[768]{0:T(1024)} %copy-done.51) | copy-start | bytes 9220
  608.4 16.9 %copy-start.54 = (f32[1024]{0:T(1024)S(1)}, f32[1024]{0:T(1024)}, u32[]{:S(2)}) copy-start(f32[1024]{0:T(1024)} %copy-done.53) | copy-start | bytes 12292
  656.5 21.1 %copy-start.20 = (bf16[512,768]{0,1:T(8,128)(2,1)S(1)}, bf16[512,768]{0,1:T(8,128)(2,1)}, u32[]{:S(2)}) copy-start(bf16[512,768]{0,1:T(8,128)(2,1)} %get-tuple-element.136) | copy-start | bytes 2359300
  679.9 212.3 %reduce-scatter.10.cloned.1.call-start = ((), (), s32[]{:S(2)}) async-start(), calls=%async_computation.17 | async-start | bytes 2433024 | tf_op jit(solution)/shard_map/reduce_scatter | solution.py:326
  696.8 17.2 %copy-start.18 = (bf16[512,768]{0,1:T(8,128)(2,1)S(1)}, bf16[512,768]{0,1:T(8,128)(2,1)}, u32[]{:S(2)}) copy-start(bf16[512,768]{0,1:T(8,128)(2,1)} %copy-done.17) | copy-start | bytes 2359300
  723.0 273.2 %reduce-scatter.8.cloned.1.call-start = ((), (), s32[]{:S(2)}) async-start(), calls=%async_computation.16 | async-start | bytes 2433024 | tf_op jit(solution)/shard_map/reduce_scatter | solution.py:325
  723.4 10.2 copy-start.2
  745.6 12.5 %copy-start.22 = (bf16[512,768]{0,1:T(8,128)(2,1)S(1)}, bf16[512,768]{0,1:T(8,128)(2,1)}, u32[]{:S(2)}) copy-start(bf16[512,768]{0,1:T(8,128)(2,1)} %copy-done.21) | copy-start | bytes 2359300
  757.9 342.9 %reduce-scatter.12.cloned.1.call-start = ((), (), s32[]{:S(2)}) async-start(), calls=%async_computation.18 | async-start | bytes 2433024 | tf_op jit(solution)/shard_map/reduce_scatter | solution.py:327
  773.8 21.4 %copy-start.30 = (bf16[12,64,1024]{2,1,0:T(8,128)(2,1)S(1)}, bf16[12,64,1024]{2,1,0:T(8,128)(2,1)}, u32[]{:S(2)}) copy-start(bf16[12,64,1024]{2,1,0:T(8,128)(2,1)} %copy-done.29) | copy-start | bytes 4718596
  805.1 16.6 %copy-start.44 = (f32[768,16]{0,1:T(8,128)S(1)}, f32[768,16]{0,1:T(8,128)}, u32[]{:S(2)}) copy-start(f32[768,16]{0,1:T(8,128)} %fusion.99) | copy-start | bytes 147460
  805.1 16.6 %copy-start.65 = (f32[768]{0:T(1024)S(1)}, f32[768]{0:T(1024)}, u32[]{:S(2)}) copy-start(f32[768]{0:T(1024)} %get-tuple-element.120) | copy-start | bytes 9220
  805.1 68.6 %copy-start.60 = (f32[1024]{0:T(1024)S(1)}, f32[1024]{0:T(1024)}, u32[]{:S(2)}) copy-start(f32[1024]{0:T(1024)} %copy-done.59) | copy-start | bytes 12292
  (48 other events, 139.3 us)
Sparse Core Ops, SparseCore 0:
  9.6 11.9 all-gather.10
  23.1 10.3 all-gather.12
  35.0 10.3 all-gather.8
  46.9 10.4 all-gather.14
  58.7 15.7 all-gather.16
  195.8 15.7 all-gather.18
  498.9 10.9 reduce-scatter.17
  563.8 13.8 reduce-scatter.15
  680.0 107.3 reduce-scatter.13
  794.0 98.2 reduce-scatter.9
  898.1 98.0 reduce-scatter.7
  1002.8 98.0 reduce-scatter.11
where the time goes:
time: 1120 us; the launch traced here: 1110 us
  matrix products  386 us (34%)
  waiting for transfers between devices  371 us (33%)
  blocking collectives  143 us (13%)
  other arithmetic  83.2 us (7%)
  local copies, waits for them, and re-layouts  80.5 us (7%)
  starting transfers between devices  28.9 us (3%)
  between operations  15.5 us (1%)
    reduce_scatter x1, waiting for transfers between devices, shards(): lax.psum_scatter(value_term, ('dp', 'expert'), scatter_dimension=0, tiled...  105 us
    reduce_scatter x1, waiting for transfers between devices, shards(): lax.psum_scatter(query_term, ('dp', 'expert'), scatter_dimension=0, tiled...  104 us
    all_to_all x1, blocking collectives, shards(): lax.all_to_all(grad_outgoing, 'expert', split_axis=0, concat_axis=0, tile...  84.9 us
    all_to_all x1, waiting for transfers between devices, shards(): lax.all_to_all(outgoing, 'expert', split_axis=0, concat_axis=0, tiled=True)  60.6 us
    dot_general x2, matrix products, masked_scores(): jnp.einsum('qhd,khd->hqk', query_block, key_seq, preferred_element_type=j...  58.9 us
    dot_general x7, matrix products, matmul_nt(): lax.dot_general(left, right, (((1,), (1,)), ((), ())), preferred_element_...  56.5 us
    all_to_all x1, waiting for transfers between devices, shards(): lax.all_to_all(produced, 'expert', split_axis=0, concat_axis=0, tiled=True)  54.4 us
    dot_general x7, matrix products, matmul(): return jnp.dot(left, right, preferred_element_type=jnp.float32)  52 us
  transfers between devices with their start and end apart: 15, of which 6 were waited for; matrix products, arithmetic and copies ran while one was open for 43% of the time, Pallas kernels for 0%

commit v1 on v0

v1 whole, which is shorter than its diff:
```python
from functools import partial

import jax
import jax.numpy as jnp
import numpy as np
from jax import lax
from jax.experimental import pallas as pl
from jax.experimental.pallas import tpu as pltpu
from jax.sharding import PartitionSpec as P

D = 768
H = 12
HD = 64
BUCKETS = 32
MAXDIST = 128
LENGTH = 1024
TILE = 128
REACH = 512
LANES = 128
epsilon = 1e-06
VMEM_LIMIT = 56 * 2**20

bf16 = jnp.bfloat16
f32 = jnp.float32
NN = (((1,), (0,)), ((), ()))
NT = (((1,), (1,)), ((), ()))
TN = (((0,), (0,)), ((), ()))


def dot(left, right, dims=NN):
    return lax.dot_general(left, right, dims, preferred_element_type=f32)


def bucket_table(length, buckets, max_reach):
    offsets = np.arange(-(length - 1), length)
    halved = buckets // 2
    linear = halved // 2
    upward = (offsets > 0).astype(np.int64) * halved
    distance = np.abs(offsets)
    scaled = (
        np.log(np.maximum(distance, 1) / linear) / np.log(max_reach / linear) * (halved - linear)
    )
    logpart = np.minimum(linear + np.floor(np.maximum(scaled, 0.0)).astype(np.int64), halved - 1)
    return (upward + np.where(distance < linear, distance, logpart)).astype(np.int32)


def bucket_onehot(offsets):
    table = bucket_table(LENGTH, BUCKETS, MAXDIST)
    return (table[offsets + LENGTH - 1][:, None] == np.arange(BUCKETS)[None, :]).astype(np.float32)


def forward_kernel(bias_ref, rows_ref, cols_ref, q_ref, k_ref, v_ref, o_ref, e_ref, r_ref, w_ref):
    low = lax.broadcasted_iota(jnp.int32, (1, LANES), 1) < HD
    blocks = LENGTH // TILE
    count = LENGTH // 2
    edge = LENGTH - 2 * TILE
    k = k_ref[...]
    v = v_ref[...]
    cols = cols_ref[...]
    for hh in range(2):
        own = low if hh == 0 else ~low
        near = bias_ref[0, hh : hh + 1, :]
        middle = pltpu.roll(
            jnp.broadcast_to(near, (TILE, REACH)), REACH - TILE, axis=1, stride=1, stride_axis=0
        )
        w_ref[:, :edge] = jnp.broadcast_to(near[:, :1], (TILE, edge))
        w_ref[:, edge : edge + 3 * TILE] = middle[:, : 3 * TILE]
        w_ref[:, edge + 3 * TILE :] = jnp.broadcast_to(near[:, REACH - 1 :], (TILE, edge))
        key = jnp.where(own, k, jnp.zeros_like(k))
        value = jnp.where(own, v, jnp.ones_like(v))
        for base in range(0, LENGTH, count):
            here = slice(base, base + count)
            starts = [TILE * (blocks - 1 - a) for a in range(base // TILE, (base + count) // TILE)]
            bias = jnp.concatenate([w_ref[:, s : s + LENGTH] for s in starts], axis=0)
            scores = dot(q_ref[here], key, NT) + bias
            scores = jnp.where(rows_ref[here] == cols, scores, -1e30)
            largest = jnp.max(scores, axis=1, keepdims=True)
            shifted = jnp.exp(scores - largest).astype(bf16)
            e_ref[hh, here, :] = shifted
            summed = dot(shifted, value)
            inverse = 1.0 / pltpu.roll(summed, HD, axis=1)
            result = (summed * inverse).astype(bf16)
            if hh == 0:
                o_ref[here] = result
                r_ref[here] = inverse
            else:
                o_ref[here] = jnp.where(low, o_ref[here], result)
                r_ref[here] = jnp.where(low, r_ref[here], inverse)


def attend(bias, rows, cols, qkv):
    pairs = D // LANES
    part = lambda at: pl.BlockSpec((LENGTH, LANES), lambda p, at=at: (0, at * pairs + p))
    return pl.pallas_call(
        forward_kernel,
        grid=(pairs,),
        in_specs=[
            pl.BlockSpec((1, 2, REACH), lambda p: (p, 0, 0)),
            pl.BlockSpec((LENGTH, 1), lambda p: (0, 0)),
            pl.BlockSpec((1, LENGTH), lambda p: (0, 0)),
            part(0),
            part(1),
            part(2),
        ],
        out_specs=[
            part(0),
            pl.BlockSpec((2, LENGTH, LENGTH), lambda p: (p, 0, 0)),
            part(0),
        ],
        out_shape=[
            jax.ShapeDtypeStruct((LENGTH, D), bf16),
            jax.ShapeDtypeStruct((H, LENGTH, LENGTH), bf16),
            jax.ShapeDtypeStruct((LENGTH, D), f32),
        ],
        scratch_shapes=[pltpu.VMEM((TILE, 2 * LENGTH - TILE), f32)],
        compiler_params=pltpu.CompilerParams(vmem_limit_bytes=VMEM_LIMIT),
        cost_estimate=pl.CostEstimate(
            flops=16 * H * LENGTH * LENGTH * HD,
            bytes_accessed=40 * 2**20,
            transcendentals=H * LENGTH * LENGTH,
        ),
        name="attend",
    )(bias, rows, cols, qkv, qkv, qkv)


def backward_kernel(
    q_ref, k_ref, v_ref, g_ref, o_ref, r_ref, e_ref, dq_ref, dk_ref, dv_ref, near_ref, t_ref
):
    lane = lax.broadcasted_iota(jnp.int32, (1, LANES), 1)
    low = lane < HD
    blocks = LENGTH // TILE
    block_of = lax.broadcasted_iota(jnp.int32, (LENGTH, LANES), 0) // TILE
    lanes = lax.broadcasted_iota(jnp.int32, (LENGTH, LANES), 1)
    q = q_ref[...]
    k = k_ref[...]
    v = v_ref[...]
    for hh in range(2):
        own = low if hh == 0 else ~low
        free = HD * (1 - hh)
        key = jnp.where(own, k, (lanes - free == block_of).astype(bf16))
        ones = jnp.where((lane == free) | (lane == free + 1), 1.0, 0.0).astype(bf16)
        value = jnp.where(own, v, ones)
        grad = jnp.where(own, g_ref[...].astype(f32) * r_ref[...], 0.0)
        term = -jnp.sum(grad * o_ref[...].astype(f32), axis=1, keepdims=True)
        grad = grad.astype(bf16)
        high = term.astype(bf16)
        rest = (term - high.astype(f32)).astype(bf16)
        joined = jnp.where(lane == free, high, jnp.where(lane == free + 1, rest, grad))
        shifted = e_ref[hh]
        ds = shifted * dot(joined, value, NT).astype(bf16)
        dq = dot(ds, key)
        t_ref[...] = jnp.zeros_like(t_ref)
        leftward = jnp.zeros((1, LANES), f32)
        rightward = jnp.zeros((1, LANES), f32)
        for a in range(blocks):
            first, last = max(a - 1, 0), min(a + 2, blocks)
            at = slice(a * TILE, (a + 1) * TILE)
            to = slice(TILE * (first - a + 1), TILE * (last - a + 1))
            t_ref[:, to] += ds[at, TILE * first : TILE * last].astype(f32)
            totals = jnp.sum(dq[at], axis=0, keepdims=True)
            block = lane - free
            leftward += jnp.where((block >= 0) & (block <= a - 2), totals, 0.0)
            rightward += jnp.where((block >= a + 2) & (block < blocks), totals, 0.0)
        dq = (dq * HD ** (-0.5)).astype(bf16)
        dv = dot(grad, shifted, TN).T.astype(bf16)
        dk = dot(q, ds, TN).T.astype(bf16)
        if hh == 0:
            dq_ref[...] = dq
            dk_ref[...] = dk
            dv_ref[...] = dv
        else:
            dq_ref[...] = jnp.where(low, dq_ref[...], dq)
            dk_ref[...] = jnp.where(low, dk_ref[...], dk)
            dv_ref[...] = jnp.where(low, dv_ref[...], dv)
        diagonals = jnp.concatenate([t_ref[...], jnp.zeros((TILE, TILE), f32)], axis=1)
        row = lax.broadcasted_iota(jnp.int32, (TILE, REACH), 0)
        for bit in range(7):
            moved = pltpu.roll(diagonals, REACH - (1 << bit), axis=1)
            diagonals = jnp.where(((row >> bit) & 1) == 1, moved, diagonals)
        at = lax.broadcasted_iota(jnp.int32, (1, REACH), 1)
        near_ref[0, hh : hh + 1, :] = (
            jnp.sum(diagonals, axis=0, keepdims=True)
            + jnp.where(at == 3 * TILE + 16, jnp.sum(leftward, axis=1, keepdims=True), 0.0)
            + jnp.where(at == 3 * TILE - 1, jnp.sum(rightward, axis=1, keepdims=True), 0.0)
        )


def attend_back(qkv, grad, heads, inverse, shifted, first, pairs):
    every = D // LANES
    part = lambda at: pl.BlockSpec((LENGTH, LANES), lambda p, at=at: (0, at * every + first + p))
    out = pl.BlockSpec((LENGTH, LANES), lambda p: (0, p))
    return pl.pallas_call(
        backward_kernel,
        grid=(pairs,),
        in_specs=[part(0), part(1), part(2), part(0), part(0), part(0)]
        + [pl.BlockSpec((2, LENGTH, LENGTH), lambda p: (first + p, 0, 0))],
        out_specs=[out, out, out]
        + [pl.BlockSpec((1, 2, REACH), lambda p: (p, 0, 0))],
        out_shape=[jax.ShapeDtypeStruct((LENGTH, pairs * LANES), bf16)] * 3
        + [jax.ShapeDtypeStruct((pairs, 2, REACH), f32)],
        scratch_shapes=[pltpu.VMEM((TILE, 3 * TILE), f32)],
        compiler_params=pltpu.CompilerParams(vmem_limit_bytes=VMEM_LIMIT),
        cost_estimate=pl.CostEstimate(
            flops=64 * pairs * LENGTH * LENGTH * HD,
            bytes_accessed=pairs * 6 * 2**20,
            transcendentals=0,
        ),
        name="attend_back",
    )(qkv, qkv, qkv, grad, heads, inverse, shifted)


def expert_kernel(
    me_ref, rows_ref, cot_ref, router_ref, up0_ref, up1_ref, down0_ref, down1_ref,
    sent_ref, back_ref, gp_ref, gl_ref, act_ref, gb_ref,
    out_ref, grow_ref, p_ref, gate_ref, *, experts, steps,
):
    step = pl.program_id(0)
    me = me_ref[0]
    lane = lax.broadcasted_iota(jnp.int32, (1, LANES), 1)

    @pl.when(step == 0)
    def _():
        logits = dot(rows_ref[...], router_ref[...])
        logits = jnp.where(lane < experts, logits, -1e30)
        weight = jnp.exp(logits - jnp.max(logits, axis=1, keepdims=True))
        p = weight / jnp.sum(weight, axis=1, keepdims=True)
        gate = experts * jnp.sum(jnp.where(lane == me, p, 0.0), axis=1, keepdims=True)
        p_ref[...] = p
        gate_ref[...] = gate
        gp_ref[...] = (gate * cot_ref[...].astype(f32)).astype(bf16)
        out_ref[...] = jnp.zeros_like(out_ref)
        grow_ref[...] = jnp.zeros_like(grow_ref)

    mine = step < steps // 2
    up = jnp.where(mine, up0_ref[...], up1_ref[...])
    down = jnp.where(mine, down0_ref[...], down1_ref[...])
    v = dot(rows_ref[...], up)
    scale = np.sqrt(2 / np.pi).astype(np.float32)
    square = v * v
    tanh = jnp.tanh(scale * v * (1.0 + 0.044715 * square))
    half = 0.5 + 0.5 * tanh
    act = (v * half).astype(bf16)
    slope = half + (0.5 * scale) * v * (1.0 - tanh * tanh) * (1.0 + (3 * 0.044715) * square)
    gb = (slope * dot(gp_ref[...], down, NT)).astype(bf16)
    act_ref[0] = act
    gb_ref[0] = gb
    out_ref[...] += dot(act, down)
    grow_ref[...] += dot(gb, up, NT)

    @pl.when(step == steps - 1)
    def _():
        gate = gate_ref[...]
        produced = out_ref[...]
        sent_ref[...] = (gate * produced).astype(bf16)
        grad_gate = jnp.sum(produced * cot_ref[...].astype(f32), axis=1, keepdims=True)
        chosen = jnp.where(lane == me, 1.0, 0.0)
        grad_logits = (grad_gate * gate * (chosen - p_ref[...])).astype(bf16)
        gl_ref[...] = grad_logits
        back_ref[...] = (grow_ref[...] + dot(grad_logits, router_ref[...], NT)).astype(bf16)


def expert_part(me, rows, cot, router, up0, up1, down0, down1, experts):
    count = rows.shape[0]
    half = up0.shape[1]
    tile = 512
    each = half // tile
    steps = 2 * each
    whole = pl.BlockSpec((count, D), lambda f: (0, 0))
    narrow = pl.BlockSpec((count, LANES), lambda f: (0, 0))
    near = lambda f: jnp.minimum(f, each - 1)
    later = lambda f: jnp.maximum(f - each, 0)
    wide = pl.BlockSpec((1, count, tile), lambda f: (f // each, 0, f % each))
    return pl.pallas_call(
        partial(expert_kernel, experts=experts, steps=steps),
        grid=(steps,),
        in_specs=[
            pl.BlockSpec(memory_space=pltpu.SMEM),
            whole,
            whole,
            pl.BlockSpec((D, LANES), lambda f: (0, 0)),
            pl.BlockSpec((D, tile), lambda f: (0, near(f))),
            pl.BlockSpec((D, tile), lambda f: (0, later(f))),
            pl.BlockSpec((tile, D), lambda f: (near(f), 0)),
            pl.BlockSpec((tile, D), lambda f: (later(f), 0)),
        ],
        out_specs=[whole, whole, whole, narrow, wide, wide],
        out_shape=[
            jax.ShapeDtypeStruct((count, D), bf16),
            jax.ShapeDtypeStruct((count, D), bf16),
            jax.ShapeDtypeStruct((count, D), bf16),
            jax.ShapeDtypeStruct((count, LANES), bf16),
            jax.ShapeDtypeStruct((2, count, half), bf16),
            jax.ShapeDtypeStruct((2, count, half), bf16),
        ],
        scratch_shapes=[
            pltpu.VMEM((count, D), f32),
            pltpu.VMEM((count, D), f32),
            pltpu.VMEM((count, LANES), f32),
            pltpu.VMEM((count, 1), f32),
        ],
        compiler_params=pltpu.CompilerParams(vmem_limit_bytes=VMEM_LIMIT),
        cost_estimate=pl.CostEstimate(
            flops=16 * count * D * half,
            bytes_accessed=30 * 2**20,
            transcendentals=2 * count * half,
        ),
        name="expert_part",
    )(me, rows, cot, router, up0, up1, down0, down1)


def shards(
    tokens,
    segments,
    routes,
    capacity,
    first_gain,
    query_weight,
    key_weight,
    value_weight,
    output_weight,
    position_bias,
    second_gain,
    router_weight,
    expert_up,
    expert_down,
    cotangent,
):
    owners = lax.axis_size("expert")
    cores = lax.axis_size("dp")
    core = lax.axis_index("dp")
    expert = lax.axis_index("expert")
    token_count = tokens.shape[0]
    experts = capacity.shape[0]
    slots = 2 * token_count // experts
    chunk = slots // 2
    swap = [(i, i ^ 1) for i in range(cores)]
    inner = 1 << ((owners.bit_length() - 1) // 2)
    outer = owners // inner
    inner_groups = [[o * inner + i for i in range(inner)] for o in range(outer)]
    outer_groups = [[o * inner + i for o in range(outer)] for i in range(inner)]
    share = D // cores // owners

    def other_core(value):
        return lax.ppermute(value, "dp", swap)

    def both(mine, other):
        return jnp.where(
            core == 0,
            jnp.concatenate([mine, other], axis=0),
            jnp.concatenate([other, mine], axis=0),
        )

    def exchange(value):
        shape = (experts, chunk, D)
        return lax.all_to_all(
            value.reshape(shape), "expert", split_axis=0, concat_axis=0, tiled=True
        ).reshape(experts * chunk, D)

    choice = routes.reshape(1, token_count)
    chosen = choice == lax.broadcasted_iota(jnp.int32, (experts, token_count), 0)
    before = (
        lax.broadcasted_iota(jnp.int32, (token_count, token_count), 0)
        < lax.broadcasted_iota(jnp.int32, (token_count, token_count), 1)
    ).astype(bf16)
    earlier = dot(chosen.astype(bf16), before)
    place = jnp.sum(jnp.where(chosen, earlier, 0.0), axis=0, keepdims=True).astype(jnp.int32)
    limit = jnp.sum(jnp.where(chosen, capacity[:, None], 0), axis=0, keepdims=True)
    kept = place < limit
    slot = choice * chunk + place % chunk
    slot_ids = lax.broadcasted_iota(jnp.int32, (experts * chunk, token_count), 0)
    picks = [
        (jnp.where(kept & (place // chunk == c), slot, -1) == slot_ids).astype(bf16)
        for c in range(2)
    ]
    picks = lax.optimization_barrier(picks)
    cot_sent = [dot(pick, cotangent).astype(bf16) for pick in picks]
    cot_rows = [exchange(rows) for rows in cot_sent]

    small = jnp.concatenate(
        [
            router_weight,
            first_gain[:, None],
            second_gain[:, None],
            jnp.zeros((D // cores, LANES - 2), bf16),
        ],
        axis=1,
    )
    mixer = jnp.concatenate([query_weight, key_weight, value_weight, output_weight], axis=1)
    mixer_full = both(mixer, other_core(mixer))
    small_full = both(small, other_core(small))
    bias_full = both(position_bias, other_core(position_bias)).astype(f32)
    up0 = expert_up[0]
    down0 = expert_down[0]
    up1 = other_core(up0)
    down1 = other_core(down0)
    router = small_full[:, :experts]
    gains = small_full[:, experts : experts + 2].astype(f32).T
    first_full = gains[0:1]
    second_full = gains[1:2]
    router_wide = jnp.pad(router, ((0, 0), (0, LANES - experts)))
    qkv_full = mixer_full[:, : 3 * D]
    output_full = mixer_full[:, 3 * D :]

    inputs = tokens.astype(f32)
    first_scale = lax.rsqrt(jnp.mean(inputs * inputs, axis=-1, keepdims=True) + epsilon)
    attn_low = (inputs * first_scale * first_full).astype(bf16)
    scaling = np.where(np.arange(3 * D) < D, HD ** (-0.5), 1.0).astype(np.float32)
    qkv = (dot(attn_low, qkv_full) * scaling[None, :]).astype(bf16)
    near = np.clip(np.arange(REACH) - REACH // 2, 1 - LENGTH, LENGTH - 1)
    bias = jnp.dot(jnp.asarray(bucket_onehot(near)), bias_full, precision=lax.Precision.HIGHEST)
    bias = bias.T.reshape(H // 2, 2, REACH)
    marks = segments.astype(f32)
    heads_low, shifted, inverse = attend(bias, marks[:, None], marks[None, :], qkv)
    hidden = inputs + dot(heads_low, output_full)
    second_scale = lax.rsqrt(jnp.mean(hidden * hidden, axis=-1, keepdims=True) + epsilon)
    ffn_low = (hidden * second_scale * second_full).astype(bf16)

    me = expert.reshape(1).astype(jnp.int32)
    ffn_low, *cot_rows = lax.optimization_barrier((ffn_low, *cot_rows))
    sent = [dot(pick, ffn_low).astype(bf16) for pick in picks]
    rows0 = exchange(sent[0])
    sent1, rows0 = lax.optimization_barrier((sent[1], rows0))
    rows1 = exchange(sent1)
    arrived = [rows0, rows1]
    parts = [
        expert_part(me, arrived[c], cot_rows[c], router_wide, up0, up1, down0, down1, experts)
        for c in range(2)
    ]
    back0 = exchange(parts[0][1])
    back_sent1, back0 = lax.optimization_barrier((parts[1][1], back0))
    back1 = exchange(back_sent1)

    def summed(left, right):
        return dot(left[0], right[0], TN) + dot(left[1], right[1], TN)

    def of_half(at, half):
        return [part[at][half] for part in parts]

    gps = [part[2] for part in parts]
    down_sent = summed(of_half(4, 1), gps).astype(bf16)
    up_sent = summed(arrived, of_half(5, 1)).astype(bf16)
    down_grad = summed(of_half(4, 0), gps) + other_core(down_sent).astype(f32)
    up_grad = summed(arrived, of_half(5, 0)) + other_core(up_sent).astype(f32)
    router_term = summed(arrived, [part[3] for part in parts])[:, :experts]

    grad_out = cotangent.astype(f32)
    grad_ffn = summed(picks, [back0, back1])
    weighted = second_full * grad_ffn
    second_term = jnp.sum(grad_ffn * hidden * second_scale, axis=0, keepdims=True)
    grad_hidden = (
        grad_out
        + second_scale * weighted
        - hidden * second_scale**3 * jnp.mean(weighted * hidden, axis=-1, keepdims=True)
    )
    grad_branch = grad_hidden.astype(bf16)
    grad_heads = dot(grad_branch, output_full, NT).astype(bf16)

    out_sent0, out_sent1, grad_heads = lax.optimization_barrier(
        (parts[0][0], parts[1][0], grad_heads)
    )
    out0 = exchange(out_sent0)
    out1 = exchange(out_sent1)
    dq, dk, dv, near_sums = attend_back(
        qkv, grad_heads, heads_low, inverse, shifted, 0, H // 2
    )
    layer_out = (hidden + summed(picks, [out0, out1])).astype(bf16)

    offsets = np.arange(REACH)
    offsets = np.where(offsets < 3 * TILE, offsets - TILE, offsets - TILE - REACH)
    bias_term = jnp.dot(
        jnp.asarray(bucket_onehot(offsets).T),
        near_sums.reshape(H, REACH).T,
        precision=lax.Precision.HIGHEST,
    )

    weights = [qkv_full[:, at * D : (at + 1) * D] for at in range(3)]
    grads = [dq, dk, dv]
    grad_attn = sum(dot(g, w, NT) for g, w in zip(grads, weights))
    weighted = first_full * grad_attn
    first_term = jnp.sum(grad_attn * inputs * first_scale, axis=0, keepdims=True)
    input_grad = (
        grad_hidden
        + first_scale * weighted
        - inputs * first_scale**3 * jnp.mean(weighted * inputs, axis=-1, keepdims=True)
    ).astype(bf16)

    order = np.arange(D).reshape(cores, outer, inner, share).transpose(0, 2, 1, 3).reshape(cores, -1)
    orders = jnp.where(core == 0, order, order[::-1])
    selector = (jnp.arange(D)[:, None, None] == orders[None]).astype(bf16)

    def halves(value):
        return [dot(value, selector[:, at]).astype(bf16) for at in range(2)]

    attn_halves = halves(attn_low)
    head_halves = halves(heads_low)

    def spread(terms, extra):
        columns = terms.shape[1]
        extra_sent = jnp.broadcast_to(extra[None], (owners,) + extra.shape)
        terms = terms.reshape(owners, share, columns)
        return jnp.concatenate([terms, extra_sent], axis=1)

    def pieces(half):
        others = [
            router_term.reshape(cores, -1, experts),
            second_term.reshape(cores, -1, 1),
            first_term.reshape(cores, -1, 1),
        ]
        others = jnp.concatenate(others, axis=2).reshape(cores, outer, inner, share, experts + 2)
        others = others.transpose(0, 2, 1, 3, 4).reshape(cores, -1, experts + 2)
        others = jnp.where((core == 0) == (half == 0), others[0], others[1])
        wide = [dot(attn_halves[half], g, TN) for g in grads]
        wide.append(dot(head_halves[half], grad_branch, TN))
        joined = jnp.concatenate(wide + [others], axis=1)
        return jnp.pad(joined, ((0, 0), (0, -joined.shape[1] % LANES)))

    columns = 4 * D + experts + 2
    columns = columns + -columns % LANES
    bias_row = jnp.pad(bias_term.reshape(1, BUCKETS * H), ((0, 0), (0, columns - BUCKETS * H)))
    other_half = jnp.concatenate([pieces(1), bias_row], axis=0).astype(bf16)
    sums = jnp.concatenate([pieces(0), bias_row], axis=0) + other_core(other_half).astype(f32)
    sums = spread(sums[:-1], sums[-1:]).astype(bf16)
    width = outer * (share + 1)
    sums = lax.all_to_all(
        sums.reshape(inner, width, columns),
        "expert",
        split_axis=0,
        concat_axis=0,
        tiled=True,
        axis_index_groups=inner_groups,
    )
    sums = jnp.sum(sums.astype(f32), axis=0).astype(bf16)
    sums = lax.all_to_all(
        sums.reshape(outer, share + 1, columns),
        "expert",
        split_axis=0,
        concat_axis=0,
        tiled=True,
        axis_index_groups=outer_groups,
    )
    sums = jnp.sum(sums.astype(f32), axis=0)
    bias_grad = sums[share, : BUCKETS * H].reshape(BUCKETS, H)
    sums = sums[:share]
    query_grad, key_grad, value_grad, output_grad = [
        sums[:, at * D : (at + 1) * D] for at in range(4)
    ]
    router_grad = sums[:, 4 * D : 4 * D + experts]
    second_grad = sums[:, 4 * D + experts]
    first_grad = sums[:, 4 * D + experts + 1]
    return (
        layer_out,
        input_grad,
        first_grad,
        query_grad,
        key_grad,
        value_grad,
        output_grad,
        bias_grad,
        second_grad,
        router_grad,
        up_grad[None],
        down_grad[None],
    )


def solution(mesh):
    both = ("dp", "expert")
    placed = (
        P(both, None),
        P(both),
        P(both, None),
        P(),
        P("dp"),
        P("dp", None),
        P("dp", None),
        P("dp", None),
        P("dp", None),
        P("dp", None),
        P("dp"),
        P("dp", None),
        P("expert", None, "dp"),
        P("expert", "dp", None),
        P(both, None),
    )
    return jax.shard_map(
        shards,
        mesh=mesh,
        in_specs=placed,
        out_specs=(
            P(both, None),
            P(both, None),
            P(both),
            P(both, None),
            P(both, None),
            P(both, None),
            P(both, None),
            P(),
            P(both),
            P(both, None),
            P("expert", None, "dp"),
            P("expert", "dp", None),
        ),
        check_vma=False,
    )
```

time: 1120 us -> 508 us (0.45)
  waiting for transfers between devices: 371 us -> 77.7 us
  matrix products: 386 us -> 154 us
  blocking collectives: 143 us -> 0 us
  Pallas kernels: 0 us -> 118 us
  local copies, waits for them, and re-layouts: 80.5 us -> 30.3 us
  starting transfers between devices: 28.9 us -> 74.5 us
  other arithmetic: 83.2 us -> 43.4 us
  between operations: 15.5 us -> 1.8 us
    dot_general x37, matrix products: 386 us -> 154 us  [the longest x35 154 us: dot(): return lax.dot_general(left, right, dims, preferred_element_type=f32)]
    reduce_scatter x6 -> x0, waiting for transfers between devices: 211 us -> none  [the longest x1 105 us: shards(): lax.psum_scatter(value_term, ('dp', 'expert'), scatter_dimension=0, tiled...]
    pallas_call x0 -> x4, Pallas kernels: none -> 118 us  [the longest x2 63.8 us: expert_part(): pl.pallas_call(partial(expert_kernel, experts=experts, steps=steps), grid...]
    all_to_all x1 -> x0, blocking collectives: 84.9 us -> none  [shards(): lax.all_to_all(grad_outgoing, 'expert', split_axis=0, concat_axis=0, tile...]
    all_to_all x3 -> x10, waiting for transfers between devices: 156 us -> 77.7 us  [the longest x8 60.6 us: exchange(): lax.all_to_all(value.reshape(shape), 'expert', split_axis=0, concat_axis=...]
    unnamed x1 -> x0, blocking collectives: 50.8 us -> none
    all_to_all x3 -> x10, starting transfers between devices: 27.9 us -> 72.9 us  [the longest x8 61.6 us: exchange(): lax.all_to_all(value.reshape(shape), 'expert', split_axis=0, concat_axis=...]
    convert_element_type x10 -> x4, other arithmetic: 48.1 us -> 6.57 us  [the longest x1 3.13 us: shards(): (jnp.where(kept & (place // chunk == c), slot, -1) == slot_ids).astype(bf16)]
  transfers between devices with their start and end apart: 15 -> 18, of which waited for: 6 -> 8; matrix products, arithmetic and copies ran while one was open for 43% -> 33% of each run, Pallas kernels for 0% -> 18%
where the time goes in v1:
time: 508 us; the launch traced here: 501 us
  matrix products  154 us (30%)
  Pallas kernels  118 us (23%)
  waiting for transfers between devices  77.7 us (15%)
  starting transfers between devices  74.5 us (15%)
  other arithmetic  43.4 us (9%)
  local copies, waits for them, and re-layouts  30.3 us (6%)
    dot_general x35, matrix products, dot(): return lax.dot_general(left, right, dims, preferred_element_type=f32)  154 us
    pallas_call x2, Pallas kernels, expert_part(): pl.pallas_call(partial(expert_kernel, experts=experts, steps=steps), grid...  63.8 us
    all_to_all x8, starting transfers between devices, exchange(): lax.all_to_all(value.reshape(shape), 'expert', split_axis=0, concat_axis=...  61.6 us
    all_to_all x8, waiting for transfers between devices, exchange(): lax.all_to_all(value.reshape(shape), 'expert', split_axis=0, concat_axis=...  60.6 us
    pallas_call x1, Pallas kernels, attend_back(): pl.pallas_call(backward_kernel, grid=(pairs,), in_specs=[part(0), part(1)...  27.5 us
    pallas_call x1, Pallas kernels, attend(): pl.pallas_call(forward_kernel, grid=(pairs,), in_specs=[pl.BlockSpec((1,...  27.2 us
    unnamed x128, local copies, waits for them, and re-layouts  13.5 us
  transfers between devices with their start and end apart: 18, of which 8 were waited for; matrix products, arithmetic and copies ran while one was open for 33% of the time, Pallas kernels for 18%

profile of v1, /device:TPU:0, one launch (start us, length us, event | category | flops | bytes accessed | tf_op | source)
XLA Modules:
  0.0 500.5 jit_solution(10453737968603442486)
XLA Ops:
  10.1 8.5 %all-to-all-start = ((bf16[16,64,768]{2,1,0:T(8,128)(2,1)}), bf16[16,64,768]{2,1,0:T(8,128)(2,1)}, u32[]{:S(2)}, u32[]{:S(2)}) async-start(bf16[16,64,768]{2,1,0:T(8,128)(2,1)} %bitcast.125), calls=%async_computation | async-start | bytes 3145728 | tf_op jit(solution)/shard_map/all_to_all | solution.py:355
  25.7 5.1 %convolution_convert_fusion.3 = bf16[1024,768]{1,0:T(8,128)(2,1)} fusion(bf16[1024,1024]{1,0:T(8,128)(2,1)} %get-tuple-element.45, bf16[1024,768]{1,0:T(8,128)(2,1)} %param.34), kind=kOutput, calls=%fused_computation.68 | convolution fusion | flops 1611399168 | bytes 5242880 | tf_op jit(solution)/shard_map/dot_general | solution.py:31
  34.8 7.8 %maximum_select_fusion = bf16[768,3072]{1,0:T(8,128)(2,1)} fusion(bf16[384,3072]{1,0:T(8,128)(2,1)} %collective-permute-done.2, bf16[384,3072]{1,0:T(8,128)(2,1)} %constant_dynamic-update-slice_fusion, pred[]{:T(512)S(6)} %eq.70), kind=kLoop, calls=%fused_computation.12 | loop fusion | flops 21233664 | bytes 9437185 | tf_op jit(solution)/shard_map/jit(_where)/select_n | solution.py:347
  42.5 10.4 %all-to-all-done = bf16[16,64,768]{2,1,0:T(8,128)(2,1)} async-done(((bf16[16,64,768]{2,1,0:T(8,128)(2,1)}), bf16[16,64,768]{2,1,0:T(8,128)(2,1)}, u32[]{:S(2)}, u32[]{:S(2)}) %all-to-all-start) | async-done | bytes 1572896 | tf_op jit(solution)/shard_map/all_to_all | solution.py:355
  52.9 8.2 %all-to-all-start.1 = ((bf16[16,64,768]{2,1,0:T(8,128)(2,1)}), bf16[16,64,768]{2,1,0:T(8,128)(2,1)}, u32[]{:S(2)}, u32[]{:S(2)}) async-start(bf16[16,64,768]{2,1,0:T(8,128)(2,1)} %bitcast.7), calls=%async_computation.1 | async-start | bytes 3145728 | tf_op jit(solution)/shard_map/all_to_all | solution.py:355
  61.1 7.8 %multiply_convert_fusion.q_ref.k_ref.v_ref = bf16[1024,2304]{1,0:T(8,128)(2,1)} fusion(f32[2304]{0:T(1024)S(1)} %copy-done.50, bf16[768,3072]{1,0:T(8,128)(2,1)} %maximum_select_fusion, bf16[1024,768]{0,1:T(8,128)(2,1)S(1)} %copy.95, f32[768]{0:T(1024)S(1)} %get-tuple-element.129, f32[1024]{0:T(1024)S(1)} %get-tuple-element.137), kind=kOutput, calls=%fused_computation | convolution fusion | flops 3631742976 | bytes 9846784 | tf_op jit(solution)/shard_map/dot_general | solution.py:31
  68.9 27.2 %attend.1 = (bf16[1024,768]{1,0:T(8,128)(2,1)}, bf16[12,1024,1024]{2,1,0:T(8,128)(2,1)}, f32[1024,768]{1,0:T(8,128)}) custom-call(f32[6,2,512]{2,1,0:T(2,128)} %reshape.244.bias_ref, f32[1024,1]{1,0:T(8,128)} %copy.99.rows_ref, f32[1,1024]{1,0:T(1,128)} %bitcast.137, bf16[1024,2304]{1,0:T(8,128)(2,1)} %multiply_convert_fusion.q_ref.k_ref.v_ref, ...), custom_call_target="tpu_custom_call" | custom-call | flops 12884901888 | bytes 41943040 | tf_op jit(solution)/shard_map/attend/pallas_call | solution.py:94
  101.5 5.1 %convolution_convert_fusion.1 = bf16[1024,768]{1,0:T(8,128)(2,1)} fusion(bf16[1024,1024]{1,0:T(8,128)(2,1)} %copy-done.18, bf16[1024,768]{0,1:T(8,128)(2,1)} %multiply_convert_fusion.1), kind=kOutput, calls=%fused_computation.66 | convolution fusion | flops 1611399168 | bytes 5242880 | tf_op jit(solution)/shard_map/dot_general | solution.py:31
  106.6 7.1 %all-to-all-start.2 = ((bf16[16,64,768]{2,1,0:T(8,128)(2,1)}), bf16[16,64,768]{2,1,0:T(8,128)(2,1)}, u32[]{:S(2)}, u32[]{:S(2)}) async-start(bf16[16,64,768]{2,1,0:T(8,128)(2,1)} %bitcast.129), calls=%async_computation.2 | async-start | bytes 3145728 | tf_op jit(solution)/shard_map/all_to_all | solution.py:355
  114.3 5.0 %convolution_convert_fusion.2 = bf16[1024,768]{1,0:T(8,128)(2,1)} fusion(bf16[1024,1024]{1,0:T(8,128)(2,1)} %get-tuple-element.45, bf16[1024,768]{0,1:T(8,128)(2,1)} %multiply_convert_fusion.1), kind=kOutput, calls=%fused_computation.67 | convolution fusion | flops 1611399168 | bytes 5242880 | tf_op jit(solution)/shard_map/dot_general | solution.py:31
  119.3 27.4 %all-to-all-done.2 = bf16[16,64,768]{2,1,0:T(8,128)(2,1)} async-done(((bf16[16,64,768]{2,1,0:T(8,128)(2,1)}), bf16[16,64,768]{2,1,0:T(8,128)(2,1)}, u32[]{:S(2)}, u32[]{:S(2)}) %all-to-all-start.2) | async-done | bytes 1572896 | tf_op jit(solution)/shard_map/all_to_all | solution.py:355
  146.7 7.5 %all-to-all-start.3 = ((bf16[16,64,768]{2,1,0:T(8,128)(2,1)}), bf16[16,64,768]{2,1,0:T(8,128)(2,1)}, u32[]{:S(2)}, u32[]{:S(2)}) async-start(bf16[16,64,768]{2,1,0:T(8,128)(2,1)} %bitcast.127), calls=%async_computation.3 | async-start | bytes 3145728 | tf_op jit(solution)/shard_map/all_to_all | solution.py:355
  155.6 31.9 %expert_part.2 = (bf16[1024,768]{1,0:T(8,128)(2,1)}, bf16[1024,768]{1,0:T(8,128)(2,1)}, bf16[1024,768]{1,0:T(8,128)(2,1)}, bf16[1024,128]{1,0:T(8,128)(2,1)}, bf...) custom-call(s32[1]{0:T(128)} %bitcast.4.me_ref, bf16[1024,768]{1,0:T(8,128)(2,1)} %bitcast.10.rows_ref, ...), custom_call_target="tpu_custom_call" | custom-call | flops 19327352832 | bytes 31457280 | tf_op jit(solution)/shard_map/expert_part/pallas_call | solution.py:273
  187.8 7.4 %all-to-all-start.4 = ((bf16[16,64,768]{2,1,0:T(8,128)(2,1)}), bf16[16,64,768]{2,1,0:T(8,128)(2,1)}, u32[]{:S(2)}, u32[]{:S(2)}) async-start(bf16[16,64,768]{2,1,0:T(8,128)(2,1)} %bitcast.128), calls=%async_computation.4 | async-start | bytes 3145728 | tf_op jit(solution)/shard_map/all_to_all | solution.py:355
  197.8 31.9 %expert_part.3 = (bf16[1024,768]{1,0:T(8,128)(2,1)}, bf16[1024,768]{1,0:T(8,128)(2,1)}, bf16[1024,768]{1,0:T(8,128)(2,1)}, bf16[1024,128]{1,0:T(8,128)(2,1)}, bf...) custom-call(s32[1]{0:T(128)} %bitcast.4.me_ref, bf16[1024,768]{1,0:T(8,128)(2,1)} %bitcast.14.rows_ref, ...), custom_call_target="tpu_custom_call" | custom-call | flops 19327352832 | bytes 31457280 | tf_op jit(solution)/shard_map/expert_part/pallas_call | solution.py:273
  229.8 7.3 %all-to-all-start.5 = ((bf16[16,64,768]{2,1,0:T(8,128)(2,1)}), bf16[16,64,768]{2,1,0:T(8,128)(2,1)}, u32[]{:S(2)}, u32[]{:S(2)}) async-start(bf16[16,64,768]{2,1,0:T(8,128)(2,1)} %bitcast.126), calls=%async_computation.5 | async-start | bytes 3145728 | tf_op jit(solution)/shard_map/all_to_all | solution.py:355
  237.5 3.7 convolution_convert_fusion.8
  248.4 5.5 %fusion.64 = f32[1024,768]{0,1:T(8,128)} fusion(bf16[1024,1024]{1,0:T(8,128)(2,1)} %copy-done.18, bf16[1024,768]{1,0:T(8,128)(2,1)} %bitcast.16), kind=kOutput, calls=%fused_computation.150 | convolution fusion | flops 1610612736 | bytes 6815744 | tf_op jit(solution)/shard_map/dot_general | solution.py:31
  253.9 7.1 %fusion.22 = f32[768,1536]{1,0:T(8,128)} fusion(bf16[1024,768]{1,0:T(8,128)(2,1)} %bitcast.14.rows_ref, bf16[2,1024,1536]{2,1,0:T(8,128)(2,1)} %get-tuple-element.69), kind=kOutput, calls=%fused_computation.41 | convolution fusion | flops 2415919104 | bytes 9437184 | tf_op jit(solution)/shard_map/dot_general | solution.py:31
  261.0 8.7 %all-to-all-done.5 = bf16[16,64,768]{2,1,0:T(8,128)(2,1)} async-done(((bf16[16,64,768]{2,1,0:T(8,128)(2,1)}), bf16[16,64,768]{2,1,0:T(8,128)(2,1)}, u32[]{:S(2)}, u32[]{:S(2)}) %all-to-all-start.5) | async-done | bytes 1572896 | tf_op jit(solution)/shard_map/all_to_all | solution.py:355
  269.7 5.7 %multiply_reduce_fusion = (f32[768]{0:T(1024)S(1)}, f32[1024]{0:T(1024)S(1)}, f32[1024,768]{0,1:T(8,128)S(1)}) fusion(f32[1024,768]{0,1:T(8,128)S(1)} %get-tuple-element.141, f32[1024]{0:T(1024)S(1)} %get-tuple-element.139, f32[768]{0:T(1024)S(1)} %get-tuple-element.128, f32[1024,768]{0,1:T(8,128)} %fusion.64, bf16[1024,1024]{1,0:T(8,128)(2,1)} %get-tuple-element.45, ...), kind=kOutput, calls=%fused_computation.55 | convolution fusion | flops 1616115968 | bytes 13121536 | tf_op jit(solution)/shard_map/dot_general | solution.py:31
  276.3 5.2 %convolution_convert_fusion.g_ref = bf16[1024,768]{1,0:T(8,128)(2,1)} fusion(bf16[768,3072]{1,0:T(8,128)(2,1)} %maximum_select_fusion, f32[1024,768]{0,1:T(8,128)S(1)} %multiply_subtract_fusion), kind=kOutput, calls=%fused_computation.65 | convolution fusion | flops 1209532416 | bytes 5898240 | tf_op jit(solution)/shard_map/dot_general | solution.py:31
  281.5 27.5 %attend_back.1 = (bf16[1024,768]{1,0:T(8,128)(2,1)}, bf16[1024,768]{1,0:T(8,128)(2,1)}, bf16[1024,768]{1,0:T(8,128)(2,1)}, f32[6,2,512]{2,1,0:T(2,128)}) custom-call(bf16[1024,2304]{1,0:T(8,128)(2,1)} %multiply_convert_fusion.q_ref.k_ref.v_ref, bf16[1024,2304]{1,0:T(8,128)(2,1)} %multiply_convert_fusion.q_ref.k_ref.v_ref, ...), custom_call_target="tpu_custom_call" | custom-call | flops 25769803776 | bytes 37748736 | tf_op jit(solution)/shard_map/attend_back/pallas_call | solution.py:192
  313.8 3.5 fusion.14
  328.0 5.2 %fusion.37 = bf16[384,3090]{1,0:T(8,128)(2,1)} fusion(bf16[384,3090]{1,0:T(8,128)(2,1)} %fusion.38, bf16[1024,768]{1,0:T(8,128)(2,1)} %get-tuple-element.43.o_ref, pred[768,2,384]{2,0,1:T(32,128)(4,1)} %copy-done.34, f32[1024,768]{0,1:T(8,128)} %copy-done.9), kind=kOutput, calls=%fused_computation.80 | convolution fusion | flops 1209434112 | bytes 5603328 | tf_op jit(solution)/shard_map/dot_general | solution.py:31
  335.4 3.5 fusion.36
  338.8 7.9 %add_convert_fusion.1 = bf16[768,1536]{1,0:T(8,128)(2,1)} fusion(f32[768,1536]{1,0:T(8,128)} %fusion.22, bf16[1024,768]{1,0:T(8,128)(2,1)} %bitcast.10.rows_ref, bf16[2,1024,1536]{2,1,0:T(8,128)(2,1)} %get-tuple-element.68), kind=kOutput, calls=%fused_computation.16 | convolution fusion | flops 2418278400 | bytes 11796480 | tf_op jit(solution)/shard_map/dot_general | solution.py:31
  347.3 4.6 fusion.15
  351.9 7.6 %all-to-all-start.6 = ((bf16[16,64,768]{2,1,0:T(8,128)(2,1)}), bf16[16,64,768]{2,1,0:T(8,128)(2,1)}, u32[]{:S(2)}, u32[]{:S(2)}) async-start(bf16[16,64,768]{2,1,0:T(8,128)(2,1)} %bitcast.124), calls=%async_computation.6 | async-start | bytes 3145728 | tf_op jit(solution)/shard_map/all_to_all | solution.py:355
  359.5 3.7 convolution_dynamic-update-slice_fusion.3
  367.7 5.4 %convolution_dynamic-update-slice_fusion = f32[384,3090]{1,0:T(8,128)} fusion(f32[384,3090]{1,0:T(8,128)} %convolution_dynamic-update-slice_fusion.1, bf16[1024,768]{1,0:T(8,128)(2,1)} %get-tuple-element.43.o_ref, pred[768,2,384]{2,0,1:T(32,128)(4,1)} %copy-done.34, f32[1024,768]{0,1:T(8,128)} %copy-done.9), kind=kOutput, calls=%fused_computation.71 | convolution fusion | flops 1209139200 | bytes 6193152 | tf_op jit(solution)/shard_map/dot_general | solution.py:31
  373.9 3.6 fusion
  379.9 4.5 convert_element_type.131
  384.4 9.4 %all-to-all-done.6 = bf16[16,64,768]{2,1,0:T(8,128)(2,1)} async-done(((bf16[16,64,768]{2,1,0:T(8,128)(2,1)}), bf16[16,64,768]{2,1,0:T(8,128)(2,1)}, u32[]{:S(2)}, u32[]{:S(2)}) %all-to-all-start.6) | async-done | bytes 1572896 | tf_op jit(solution)/shard_map/all_to_all | solution.py:355
  393.8 5.0 all-to-all-start.8
  398.8 8.0 %add_convert_fusion = bf16[1536,768]{1,0:T(8,128)(2,1)} fusion(f32[1536,768]{1,0:T(8,128)} %fusion.15, bf16[1024,768]{1,0:T(8,128)(2,1)} %get-tuple-element.71, bf16[2,1024,1536]{2,1,0:T(8,128)(2,1)} %get-tuple-element.70), kind=kOutput, calls=%fused_computation.14 | convolution fusion | flops 2418278400 | bytes 11796480 | tf_op jit(solution)/shard_map/dot_general | solution.py:31
  406.8 6.8 %fusion.20 = f32[1536,768]{1,0:T(8,128)} fusion(bf16[1024,768]{1,0:T(8,128)(2,1)S(1)} %copy-done.51, bf16[2,1024,1536]{2,1,0:T(8,128)(2,1)} %get-tuple-element.70), kind=kOutput, calls=%fused_computation.39 | convolution fusion | flops 2415919104 | bytes 9437184 | tf_op jit(solution)/shard_map/dot_general | solution.py:31
  413.6 7.2 %fusion.25 = f32[768,1536]{1,0:T(8,128)} fusion(bf16[1024,768]{1,0:T(8,128)(2,1)} %bitcast.14.rows_ref, bf16[2,1024,1536]{2,1,0:T(8,128)(2,1)} %get-tuple-element.69), kind=kOutput, calls=%fused_computation.44 | convolution fusion | flops 2415919104 | bytes 9437184 | tf_op jit(solution)/shard_map/dot_general | solution.py:31
  420.8 8.4 %all-to-all-done.8 = bf16[4,100,3200]{2,1,0:T(8,128)(2,1)} async-done(((bf16[4,100,3200]{2,1,0:T(8,128)(2,1)}), bf16[4,100,3200]{2,1,0:T(8,128)(2,1)}, u32[]{:S(2)}, u32[]{:S(2)}) %all-to-all-start.8) | async-done | bytes 2560032 | tf_op jit(solution)/shard_map/all_to_all | solution.py:524
  429.2 8.0 %all-to-all-start.7 = ((bf16[16,64,768]{2,1,0:T(8,128)(2,1)}), bf16[16,64,768]{2,1,0:T(8,128)(2,1)}, u32[]{:S(2)}, u32[]{:S(2)}) async-start(bf16[16,64,768]{2,1,0:T(8,128)(2,1)} %bitcast.123), calls=%async_computation.7 | async-start | bytes 3145728 | tf_op jit(solution)/shard_map/all_to_all | solution.py:355
  437.2 5.3 %fusion.18 = f32[1536,768]{1,0:T(8,128)S(1)} fusion(bf16[1024,768]{1,0:T(8,128)(2,1)} %get-tuple-element.73, bf16[2,1024,1536]{2,1,0:T(8,128)(2,1)} %get-tuple-element.72), kind=kOutput, calls=%fused_computation.37 | convolution fusion | flops 2415919104 | bytes 9437184 | tf_op jit(solution)/shard_map/dot_general | solution.py:31
  442.5 8.2 %add_bitcast_fusion.1 = f32[1,768,1536]{2,1,0:T(8,128)} fusion(bf16[768,1536]{1,0:T(8,128)(2,1)} %collective-permute-done.6, f32[768,1536]{1,0:T(8,128)S(1)} %copy-done.17, bf16[1024,768]{1,0:T(8,128)(2,1)} %bitcast.10.rows_ref, bf16[2,1024,1536]{2,1,0:T(8,128)(2,1)} %get-tuple-element.68), kind=kOutput, calls=%fused_computation.15 | convolution fusion | flops 2419458048 | bytes 16515072 | tf_op jit(solution)/shard_map/dot_general | solution.py:31
  450.8 4.9 add_bitcast_fusion
  465.7 4.4 all-to-all-done.7
  470.1 6.3 %all-to-all-start.9 = ((bf16[4,25,3200]{2,1,0:T(8,128)(2,1)}), bf16[4,25,3200]{2,1,0:T(8,128)(2,1)}, u32[]{:S(2)}, u32[]{:S(2)}) async-start(bf16[4,25,3200]{2,1,0:T(8,128)(2,1)} %reshape.265), calls=%async_computation.9 | async-start | bytes 1638400 | tf_op jit(solution)/shard_map/all_to_all | solution.py:533
  476.3 4.0 fusion.65
  480.4 4.5 add_convert_fusion.2
  487.4 8.7 %all-to-all-done.9 = bf16[4,25,3200]{2,1,0:T(8,128)(2,1)} async-done(((bf16[4,25,3200]{2,1,0:T(8,128)(2,1)}), bf16[4,25,3200]{2,1,0:T(8,128)(2,1)}, u32[]{:S(2)}, u32[]{:S(2)}) %all-to-all-start.9) | async-done | bytes 640032 | tf_op jit(solution)/shard_map/all_to_all | solution.py:533
  (219 shorter events, 81.4 us)
Async XLA Ops:
  0.6 6.5 %copy-start.20 = (bf16[1024,768]{1,0:T(8,128)(2,1)S(1)}, bf16[1024,768]{1,0:T(8,128)(2,1)}, u32[]{:S(2)}) copy-start(bf16[1024,768]{1,0:T(8,128)(2,1)} %param.34) | copy-start | bytes 4718596
  10.1 8.5 %copy-start.30 = (bf16[384,768]{1,0:T(8,128)(2,1)S(1)}, bf16[384,768]{1,0:T(8,128)(2,1)}, u32[]{:S(2)}) copy-start(bf16[384,768]{1,0:T(8,128)(2,1)} %param.25) | copy-start | bytes 1769476
  10.1 9.4 %copy-start.31 = (bf16[384,768]{1,0:T(8,128)(2,1)S(1)}, bf16[384,768]{1,0:T(8,128)(2,1)}, u32[]{:S(2)}) copy-start(bf16[384,768]{1,0:T(8,128)(2,1)} %param.26) | copy-start | bytes 1769476
  10.1 10.3 %copy-start.32 = (bf16[384,768]{1,0:T(8,128)(2,1)S(1)}, bf16[384,768]{1,0:T(8,128)(2,1)}, u32[]{:S(2)}) copy-start(bf16[384,768]{1,0:T(8,128)(2,1)} %param.27) | copy-start | bytes 1769476
  10.1 42.8 %all-to-all-start = ((bf16[16,64,768]{2,1,0:T(8,128)(2,1)}), bf16[16,64,768]{2,1,0:T(8,128)(2,1)}, u32[]{:S(2)}, u32[]{:S(2)}) async-start(bf16[16,64,768]{2,1,0:T(8,128)(2,1)} %bitcast.125), calls=%async_computation | async-start | bytes 3145728 | tf_op jit(solution)/shard_map/all_to_all | solution.py:355
  22.1 12.6 %collective-permute-start.2 = (bf16[384,3072]{1,0:T(8,128)(2,1)}, bf16[384,3072]{1,0:T(8,128)(2,1)}, u32[]{:S(2)}, u32[]{:S(2)}) collective-permute-start(bf16[384,3072]{1,0:T(8,128)(2,1)} %constant_dynamic-update-slice_fusion), channel_id=1, source_target_pairs={{0,16},{16,0},{1,17},{17,1},{2,18},{18,2},{3,19},{19,3},{4,20},{20... | collective-permute-start | bytes 7077896 | tf_op jit(solution)/shard_map/ppermute | solution.py:344
  22.2 9.6 %collective-permute-start = (bf16[16,12]{1,0:T(8,128)(2,1)S(1)}, bf16[16,12]{1,0:T(8,128)(2,1)S(1)}, u32[]{:S(2)}, u32[]{:S(2)}) collective-permute-start(bf16[16,12]{1,0:T(8,128)(2,1)S(1)} %copy-done.44), channel_id=1, source_target_pairs={{0,16},{16,0},{1,17},{17,1},{2,18},{18,2},{3,19},{19,3},{4,20},{20... | collective-permute-start | bytes 1160 | tf_op jit(solution)/shard_map/ppermute | solution.py:344
  23.4 9.3 %collective-permute-start.1 = (bf16[384,144]{1,0:T(8,128)(2,1)S(1)}, bf16[384,144]{1,0:T(8,128)(2,1)}, u32[]{:S(2)}, u32[]{:S(2)}) collective-permute-start(bf16[384,144]{1,0:T(8,128)(2,1)S(1)} %pad_maximum_fusion.1), channel_id=1, source_target_pairs={{0,16},{16,0},{1,17},{17,1},{2,18},{18,2},{3,19},{19,3},{4,20},{20... | collective-permute-start | bytes 331784 | tf_op jit(solution)/shard_map/ppermute | solution.py:344
  24.5 36.6 %copy-start = (bf16[1024,768]{0,1:T(8,128)(2,1)}, bf16[1024,768]{0,1:T(8,128)(2,1)S(1)}, u32[]{:S(2)}) copy-start(bf16[1024,768]{0,1:T(8,128)(2,1)S(1)} %copy.95) | copy-start | bytes 4718596
  25.6 6.2 %copy-start.37 = (f32[512,32]{1,0:T(8,128)S(1)}, f32[512,32]{1,0:T(8,128)}, u32[]{:S(2)}) copy-start(f32[512,32]{1,0:T(8,128)} %constant.75.clone) | copy-start | bytes 196612
  25.6 7.1 %copy-start.22 = (bf16[384,1]{1,0:T(8,128)(2,1)S(1)}, bf16[384,1]{1,0:T(8,128)(2,1)}, u32[]{:S(2)}) copy-start(bf16[384,1]{1,0:T(8,128)(2,1)} %copy-done.21) | copy-start | bytes 2308
  25.6 7.1 %copy-start.24 = (bf16[384,1]{1,0:T(8,128)(2,1)S(1)}, bf16[384,1]{1,0:T(8,128)(2,1)}, u32[]{:S(2)}) copy-start(bf16[384,1]{1,0:T(8,128)(2,1)} %copy-done.23) | copy-start | bytes 2308
  25.6 7.1 %copy-start.26 = (bf16[384,16]{1,0:T(8,128)(2,1)S(1)}, bf16[384,16]{1,0:T(8,128)(2,1)}, u32[]{:S(2)}) copy-start(bf16[384,16]{1,0:T(8,128)(2,1)} %copy-done.25) | copy-start | bytes 36868
  25.6 7.1 %copy-start.28 = (bf16[384,126]{1,0:T(8,128)(2,1)S(1)}, bf16[384,126]{1,0:T(8,128)(2,1)}, u32[]{:S(2)}) copy-start(bf16[384,126]{1,0:T(8,128)(2,1)} %copy-done.27) | copy-start | bytes 290308
  30.7 11.8 %copy-start.42 = (f32[1024]{0:T(1024)}, f32[1024]{0:T(1024)S(1)}, u32[]{:S(2)}) copy-start(f32[1024]{0:T(1024)S(1)} %convert_element_type.110) | copy-start | bytes 12292
  42.5 18.6 %copy-start.50 = (f32[2304]{0:T(1024)S(1)}, f32[2304]{0:T(1024)}, u32[]{:S(2)}) copy-start(f32[2304]{0:T(1024)} %constant.87) | copy-start | bytes 27652
  52.9 48.6 %all-to-all-start.1 = ((bf16[16,64,768]{2,1,0:T(8,128)(2,1)}), bf16[16,64,768]{2,1,0:T(8,128)(2,1)}, u32[]{:S(2)}, u32[]{:S(2)}) async-start(bf16[16,64,768]{2,1,0:T(8,128)(2,1)} %bitcast.7), calls=%async_computation.1 | async-start | bytes 3145728 | tf_op jit(solution)/shard_map/all_to_all | solution.py:355
  68.9 27.2 %copy-start.1 = (bf16[1024,768]{0,1:T(8,128)(2,1)S(1)}, bf16[1024,768]{0,1:T(8,128)(2,1)}, u32[]{:S(2)}) copy-start(bf16[1024,768]{0,1:T(8,128)(2,1)} %copy-done) | copy-start | bytes 4718596
  106.6 40.1 %all-to-all-start.2 = ((bf16[16,64,768]{2,1,0:T(8,128)(2,1)}), bf16[16,64,768]{2,1,0:T(8,128)(2,1)}, u32[]{:S(2)}, u32[]{:S(2)}) async-start(bf16[16,64,768]{2,1,0:T(8,128)(2,1)} %bitcast.129), calls=%async_computation.2 | async-start | bytes 3145728 | tf_op jit(solution)/shard_map/all_to_all | solution.py:355
  113.7 41.9 %collective-permute-start.3 = (bf16[768,1536]{1,0:T(8,128)(2,1)}, bf16[768,1536]{1,0:T(8,128)(2,1)}, u32[]{:S(2)}, u32[]{:S(2)}) collective-permute-start(bf16[768,1536]{1,0:T(8,128)(2,1)} %bitcast.138), channel_id=1, source_target_pairs={{0,16},{16,0},{1,17},{17,1},{2,18},{18,2},{3,19},{19,3},{4,20},{20... | collective-permute-start | bytes 7077896 | tf_op jit(solution)/shard_map/ppermute | solution.py:344
  113.8 41.8 %collective-permute-start.4 = (bf16[1536,768]{1,0:T(8,128)(2,1)}, bf16[1536,768]{1,0:T(8,128)(2,1)}, u32[]{:S(2)}, u32[]{:S(2)}) collective-permute-start(bf16[1536,768]{1,0:T(8,128)(2,1)} %bitcast.141), channel_id=1, source_target_pairs={{0,16},{16,0},{1,17},{17,1},{2,18},{18,2},{3,19},{19,3},{4,20},{20... | collective-permute-start | bytes 7077896 | tf_op jit(solution)/shard_map/ppermute | solution.py:344
  146.7 41.1 %all-to-all-start.3 = ((bf16[16,64,768]{2,1,0:T(8,128)(2,1)}), bf16[16,64,768]{2,1,0:T(8,128)(2,1)}, u32[]{:S(2)}, u32[]{:S(2)}) async-start(bf16[16,64,768]{2,1,0:T(8,128)(2,1)} %bitcast.127), calls=%async_computation.3 | async-start | bytes 3145728 | tf_op jit(solution)/shard_map/all_to_all | solution.py:355
  187.8 41.9 %all-to-all-start.4 = ((bf16[16,64,768]{2,1,0:T(8,128)(2,1)}), bf16[16,64,768]{2,1,0:T(8,128)(2,1)}, u32[]{:S(2)}, u32[]{:S(2)}) async-start(bf16[16,64,768]{2,1,0:T(8,128)(2,1)} %bitcast.128), calls=%async_computation.4 | async-start | bytes 3145728 | tf_op jit(solution)/shard_map/all_to_all | solution.py:355
  229.7 7.4 %copy-start.46 = (s32[2,384]{1,0:T(2,128)S(1)}, s32[2,384]{1,0:T(2,128)}, u32[]{:S(2)}) copy-start(s32[2,384]{1,0:T(2,128)} %constant.77.clone) | copy-start | bytes 9220
  229.7 7.4 %copy-start.47 = (s32[2,384]{1,0:T(2,128)S(1)}, s32[2,384]{1,0:T(2,128)}, u32[]{:S(2)}) copy-start(s32[2,384]{1,0:T(2,128)} %constant.78.clone) | copy-start | bytes 9220
  229.8 39.9 %all-to-all-start.5 = ((bf16[16,64,768]{2,1,0:T(8,128)(2,1)}), bf16[16,64,768]{2,1,0:T(8,128)(2,1)}, u32[]{:S(2)}, u32[]{:S(2)}) async-start(bf16[16,64,768]{2,1,0:T(8,128)(2,1)} %bitcast.126), calls=%async_computation.5 | async-start | bytes 3145728 | tf_op jit(solution)/shard_map/all_to_all | solution.py:355
  269.7 5.7 %copy-start.16 = (bf16[1024,768]{0,1:T(8,128)(2,1)S(1)}, bf16[1024,768]{0,1:T(8,128)(2,1)}, u32[]{:S(2)}) copy-start(bf16[1024,768]{0,1:T(8,128)(2,1)} %copy.100) | copy-start | bytes 4718596
  269.7 5.7 %copy-start.41 = (f32[1024]{0:T(1024)S(1)}, f32[1024]{0:T(1024)}, u32[]{:S(2)}) copy-start(f32[1024]{0:T(1024)} %get-tuple-element.138) | copy-start | bytes 12292
  276.3 32.7 %slice-start = ((s8[4718592]{0:T(1024)(128)(4,1)}), s8[4194304]{0:T(1024)(128)(4,1)S(1)}, s32[]{:S(2)}) async-start(s8[4718592]{0:T(1024)(128)(4,1)} %bitcast.119), calls=%async_computation.10 | async-start | bytes 8388608
  281.5 27.5 %slice-start.1 = ((s8[4718592]{0:T(1024)(128)(4,1)}), s8[524288]{0:T(1024)(128)(4,1)S(1)}, s32[]{:S(2)}) async-start(s8[4718592]{0:T(1024)(128)(4,1)} %bitcast.119), calls=%async_computation.11 | async-start | bytes 1048576
  313.8 5.7 %copy-start.39 = (f32[6,2,512]{2,1,0:T(2,128)S(1)}, f32[6,2,512]{2,1,0:T(2,128)}, u32[]{:S(2)}) copy-start(f32[6,2,512]{2,1,0:T(2,128)} %get-tuple-element.67) | copy-start | bytes 73732
  313.8 5.7 %copy-start.38 = (f32[32,512]{1,0:T(8,128)S(1)}, f32[32,512]{1,0:T(8,128)}, u32[]{:S(2)}) copy-start(f32[32,512]{1,0:T(8,128)} %constant.76.clone) | copy-start | bytes 196612
  319.9 6.5 %copy-start.6 = (bf16[1024,768]{1,0:T(8,128)(2,1)S(1)}, bf16[1024,768]{1,0:T(8,128)(2,1)}, u32[]{:S(2)}) copy-start(bf16[1024,768]{1,0:T(8,128)(2,1)} %get-tuple-element.64) | copy-start | bytes 4718596
  335.3 12.0 %slice-start.4 = ((s8[6291456]{0:T(1024)(128)(4,1)}), s8[4194304]{0:T(1024)(128)(4,1)S(1)}, s32[]{:S(2)}) async-start(s8[6291456]{0:T(1024)(128)(4,1)} %bitcast.144), calls=%async_computation.14 | async-start | bytes 8388608
  338.8 35.1 %collective-permute-start.5 = (bf16[385,3200]{1,0:T(8,128)(2,1)}, bf16[385,3200]{1,0:T(8,128)(2,1)}, u32[]{:S(2)}, u32[]{:S(2)}) collective-permute-start(bf16[385,3200]{1,0:T(8,128)(2,1)} %fusion.36), channel_id=1, source_target_pairs={{0,16},{16,0},{1,17},{17,1},{2,18},{18,2},{3,19},{19,3},{4,20},{20... | collective-permute-start | bytes 7392008 | tf_op jit(solution)/shard_map/ppermute | solution.py:344
  338.8 8.5 %slice-start.5 = ((s8[6291456]{0:T(1024)(128)(4,1)}), s8[2097152]{0:T(1024)(128)(4,1)S(1)}, s32[]{:S(2)}) async-start(s8[6291456]{0:T(1024)(128)(4,1)} %bitcast.144), calls=%async_computation.15 | async-start | bytes 4194304
  338.8 8.5 %copy-start.52 = (bf16[1024,768]{1,0:T(8,128)(2,1)S(1)}, bf16[1024,768]{1,0:T(8,128)(2,1)}, u32[]{:S(2)}) copy-start(bf16[1024,768]{1,0:T(8,128)(2,1)} %get-tuple-element.73) | copy-start | bytes 4718596
  346.8 95.7 %collective-permute-start.6 = (bf16[768,1536]{1,0:T(8,128)(2,1)}, bf16[768,1536]{1,0:T(8,128)(2,1)}, u32[]{:S(2)}, u32[]{:S(2)}) collective-permute-start(bf16[768,1536]{1,0:T(8,128)(2,1)} %add_convert_fusion.1), channel_id=1, source_target_pairs={{0,16},{16,0},{1,17},{17,1},{2,18},{18,2},{3,19},{19,3},{4,20},{20... | collective-permute-start | bytes 7077896 | tf_op jit(solution)/shard_map/ppermute | solution.py:344
  351.9 41.9 %all-to-all-start.6 = ((bf16[16,64,768]{2,1,0:T(8,128)(2,1)}), bf16[16,64,768]{2,1,0:T(8,128)(2,1)}, u32[]{:S(2)}, u32[]{:S(2)}) async-start(bf16[16,64,768]{2,1,0:T(8,128)(2,1)} %bitcast.124), calls=%async_computation.6 | async-start | bytes 3145728 | tf_op jit(solution)/shard_map/all_to_all | solution.py:355
  367.7 5.4 %copy-start.29 = (f32[1,4,4,24,18]{4,3,2,1,0:T(8,128)S(1)}, f32[1,4,4,24,18]{4,3,2,1,0:T(8,128)}, u32[]{:S(2)}) copy-start(f32[1,4,4,24,18]{4,3,2,1,0:T(8,128)} %slice_select_fusion.1) | copy-start | bytes 82948
  393.8 35.4 %all-to-all-start.8 = ((bf16[4,100,3200]{2,1,0:T(8,128)(2,1)}), bf16[4,100,3200]{2,1,0:T(8,128)(2,1)}, u32[]{:S(2)}, u32[]{:S(2)}) async-start(bf16[4,100,3200]{2,1,0:T(8,128)(2,1)} %convert_element_type.131), calls=%async_computation.8 | async-start | bytes 5324800 | tf_op jit(solution)/shard_map/all_to_all | solution.py:524
  398.8 8.0 %copy-start.51 = (bf16[1024,768]{1,0:T(8,128)(2,1)S(1)}, bf16[1024,768]{1,0:T(8,128)(2,1)}, u32[]{:S(2)}) copy-start(bf16[1024,768]{1,0:T(8,128)(2,1)} %get-tuple-element.71) | copy-start | bytes 4718596
  406.8 44.0 %collective-permute-start.7 = (bf16[1536,768]{1,0:T(8,128)(2,1)}, bf16[1536,768]{1,0:T(8,128)(2,1)}, u32[]{:S(2)}, u32[]{:S(2)}) collective-permute-start(bf16[1536,768]{1,0:T(8,128)(2,1)} %add_convert_fusion), channel_id=1, source_target_pairs={{0,16},{16,0},{1,17},{17,1},{2,18},{18,2},{3,19},{19,3},{4,20},{20... | collective-permute-start | bytes 7077896 | tf_op jit(solution)/shard_map/ppermute | solution.py:344
  429.2 40.9 %all-to-all-start.7 = ((bf16[16,64,768]{2,1,0:T(8,128)(2,1)}), bf16[16,64,768]{2,1,0:T(8,128)(2,1)}, u32[]{:S(2)}, u32[]{:S(2)}) async-start(bf16[16,64,768]{2,1,0:T(8,128)(2,1)} %bitcast.123), calls=%async_computation.7 | async-start | bytes 3145728 | tf_op jit(solution)/shard_map/all_to_all | solution.py:355
  437.2 5.3 %copy-start.17 = (f32[768,1536]{1,0:T(8,128)S(1)}, f32[768,1536]{1,0:T(8,128)}, u32[]{:S(2)}) copy-start(f32[768,1536]{1,0:T(8,128)} %fusion.25) | copy-start | bytes 14155780
  437.2 13.6 %slice-start.2 = ((s8[4718592]{0:T(1024)(128)(4,1)}), s8[4194304]{0:T(1024)(128)(4,1)S(1)}, s32[]{:S(2)}) async-start(s8[4718592]{0:T(1024)(128)(4,1)} %bitcast.121), calls=%async_computation.12 | async-start | bytes 8388608
  442.5 8.3 %slice-start.3 = ((s8[4718592]{0:T(1024)(128)(4,1)}), s8[524288]{0:T(1024)(128)(4,1)S(1)}, s32[]{:S(2)}) async-start(s8[4718592]{0:T(1024)(128)(4,1)} %bitcast.121), calls=%async_computation.13 | async-start | bytes 1048576
  470.1 26.0 %all-to-all-start.9 = ((bf16[4,25,3200]{2,1,0:T(8,128)(2,1)}), bf16[4,25,3200]{2,1,0:T(8,128)(2,1)}, u32[]{:S(2)}, u32[]{:S(2)}) async-start(bf16[4,25,3200]{2,1,0:T(8,128)(2,1)} %reshape.265), calls=%async_computation.9 | async-start | bytes 1638400 | tf_op jit(solution)/shard_map/all_to_all | solution.py:533
  (29 other events, 97.1 us)
